TPU v7x, 32 devices: a whole 2x2x4 slice. The times are simulated.
32 devices in a mesh: parts: 2 (over x), pos: 8 (over z, y), slab: 2 (over core).
Axes of the slice: x: 2, y: 2, z: 4, core: 2. Of those that a mesh axis runs over, the one named last changes fastest.
Arguments:
- obj_real: float32 [8, 2048, 1024], P(('parts', 'slab'), 'pos'), parts along dimension 0, may hold values from 0.5 to 1.5
- obj_imag: float32 [8, 2048, 1024], P(('parts', 'slab'), 'pos'), parts along dimension 0, may hold values from -1.5 to 1.5
- probe: float32 [2, 256, 256], replicated, may hold values from -5 to 5
- taps: float32 [2, 63], replicated, may hold values from -1.3 to 1.3
- intensity: float32 [32, 256, 256], P(('parts', 'pos')), parts along dimension 0, may hold values from 0.25 to 8
- row_off: int32 [32], P(('parts', 'pos')), parts along dimension 0, may hold values from 0 to 255
- col_off: int32 [32], P(('parts', 'pos')), parts along dimension 0, may hold values from 0 to 768
Outputs:
- grad_real: float32 [8, 2048, 1024], P(('parts', 'slab'), 'pos'), parts along dimension 0
- grad_imag: float32 [8, 2048, 1024], P(('parts', 'slab'), 'pos'), parts along dimension 0
There are 2 independent parts, one for each index of `parts`. A program takes and returns all parts, laid end to end along the dimension named above; an argument that names none is the same for every part. Nothing has to cross between parts.
All inputs are finite; a program needn't handle non-finite values.
Results may differ from a plain program's by a relative error of at most 0.0003.
Values sent between devices are 32-bit elements; how exact they have to be, the bound alone decides.
A program may use at most 128 MiB of HBM per device.

v0:
```python
import math

import jax
import jax.numpy as jnp
from jax import lax
from jax.sharding import PartitionSpec as P

HIGH = lax.Precision.HIGHEST


def from_behind(block, axis, distance):
    devices = range(lax.axis_size(axis))
    route = [((i - distance) % len(devices), i) for i in devices]
    return lax.ppermute(block, axis, route)


def shifted(x, axis, by):
    count = lax.axis_size(axis)
    pairs = [(i, i + by) for i in range(count) if 0 <= i + by < count]
    return lax.ppermute(x, axis, pairs)


def cprod(form, ar, ai, br, bi):

    def mul(left, right):
        return jnp.einsum(form, left, right, precision=HIGH, preferred_element_type=jnp.float32)

    return (mul(ar, br) - mul(ai, bi), mul(ar, bi) + mul(ai, br))


def band(taps, width):
    rows = jnp.arange(width, dtype=jnp.int32)[:, None]
    cols = jnp.arange(width, dtype=jnp.int32)[None, :]
    offset = cols - rows
    half = (taps.shape[1] - 1) // 2
    index = jnp.clip(offset + half, 0, taps.shape[1] - 1)
    inside = jnp.abs(offset) <= half
    return (jnp.where(inside, taps[0][index], 0.0), jnp.where(inside, taps[1][index], 0.0))


def fourier(width):
    steps = jnp.arange(width, dtype=jnp.int32)
    phase = steps[:, None] * steps[None, :] % width
    angle = 2.0 * math.pi / width * phase.astype(jnp.float32)
    norm = 1.0 / math.sqrt(width)
    return (jnp.cos(angle) * norm, -jnp.sin(angle) * norm)


def propagate(kr, ki, xr, xi):
    left = cprod("ij,bjk->bik", kr, ki, xr, xi)
    return cprod("bij,kj->bik", left[0], left[1], kr, ki)


def adjoint_prop(kr, ki, xr, xi):
    left = cprod("ji,bjk->bik", kr, -ki, xr, xi)
    return cprod("bij,jk->bik", left[0], left[1], kr, -ki)


def target_amplitude(
    exit_wave_real, exit_wave_imaginary, measured_pattern, wave_real, wave_imaginary
):
    left = cprod("ij,bjk->bik", wave_real, wave_imaginary, exit_wave_real, exit_wave_imaginary)
    farfield_real, farfield_imaginary = cprod(
        "bij,jk->bik", left[0], left[1], wave_real, wave_imaginary
    )
    amplitude_residual = (
        farfield_real * farfield_real + farfield_imaginary * farfield_imaginary - measured_pattern
    )
    grad_r = 2.0 * amplitude_residual * farfield_real
    grad_i = 2.0 * amplitude_residual * farfield_imaginary
    back = cprod("ij,bjk->bik", wave_real, -wave_imaginary, grad_r, grad_i)
    return cprod("bij,jk->bik", back[0], back[1], wave_real, -wave_imaginary)


def cut(ext_r, ext_i, rows, cols, width):
    depth = ext_r.shape[0]
    zero = jnp.zeros((), jnp.int32)

    def one(row, col):
        start = (zero, row, col)
        return (
            lax.dynamic_slice(ext_r, start, (depth, width, width)),
            lax.dynamic_slice(ext_i, start, (depth, width, width)),
        )

    return jax.vmap(one)(rows, cols)


def forward_pass(src_r, src_i, pat_r, pat_i, kr, ki):
    waves_r, waves_i = ([], [])
    cur_r, cur_i = (src_r, src_i)
    for level in range(pat_r.shape[1]):
        waves_r.append(cur_r)
        waves_i.append(cur_i)
        o_r = pat_r[:, level]
        o_i = pat_i[:, level]
        cur_r, cur_i = propagate(kr, ki, cur_r * o_r - cur_i * o_i, cur_r * o_i + cur_i * o_r)
    return (jnp.stack(waves_r, 1), jnp.stack(waves_i, 1), cur_r, cur_i)


def backward_pass(chirp_real, chirp_imaginary, waves_r, waves_i, pat_r, pat_i, kr, ki):
    depth = pat_r.shape[1]
    terms_r = [None] * depth
    terms_i = [None] * depth
    for level in reversed(range(depth)):
        a_r, a_i = adjoint_prop(kr, ki, chirp_real, chirp_imaginary)
        w_r = waves_r[:, level]
        w_i = waves_i[:, level]
        terms_r[level] = a_r * w_r + a_i * w_i
        terms_i[level] = a_i * w_r - a_r * w_i
        o_r = pat_r[:, level]
        o_i = pat_i[:, level]
        chirp_real, chirp_imaginary = (a_r * o_r + a_i * o_i, a_i * o_r - a_r * o_i)
    return (chirp_real, chirp_imaginary, jnp.stack(terms_r, 1), jnp.stack(terms_i, 1))


def deposit(acc_r, acc_i, term_r, term_i, rows, cols):
    depth, width = (term_r.shape[1], term_r.shape[2])
    zero = jnp.zeros((), jnp.int32)

    def add_one(item, state):
        total_r, total_i = state
        start = (zero, rows[item], cols[item])
        now_r = lax.dynamic_slice(total_r, start, (depth, width, width))
        now_i = lax.dynamic_slice(total_i, start, (depth, width, width))
        total_r = lax.dynamic_update_slice(total_r, now_r + term_r[item], start)
        total_i = lax.dynamic_update_slice(total_i, now_i + term_i[item], start)
        return (total_r, total_i)

    return lax.fori_loop(0, term_r.shape[0], add_one, (acc_r, acc_i))


def place(whole, fresh, start, valid):
    older = lax.dynamic_slice_in_dim(whole, start, fresh.shape[0], 0)
    return lax.dynamic_update_slice_in_dim(whole, jnp.where(valid, fresh, older), start, 0)


def local(obj_real, obj_imag, probe, taps, intensity, row_off, col_off):
    width = probe.shape[-1]
    count = intensity.shape[0]
    cols_all = obj_real.shape[2]
    kr, ki = band(taps, width)
    wave_real, wave_imaginary = fourier(width)
    nslab = lax.axis_size("slab")
    section = lax.axis_index("slab")
    depth = obj_real.shape[0]
    below_r, below_i = from_behind((obj_real, obj_imag), "pos", -1)
    ext_r = jnp.concatenate([obj_real, below_r], axis=1)
    ext_i = jnp.concatenate([obj_imag, below_i], axis=1)
    pat_r, pat_i = cut(ext_r, ext_i, row_off, col_off, width)
    groups = 1
    size = count // groups
    ticks = groups + nslab - 1
    lead_r = jnp.broadcast_to(probe[0], (size, width, width))
    lead_i = jnp.broadcast_to(probe[1], (size, width, width))
    field = jnp.zeros((size, width, width), jnp.float32)
    stored = jnp.zeros((count, depth, width, width), jnp.float32)
    exits = jnp.zeros((count, width, width), jnp.float32)

    def forward_tick(tick, carry):
        store_r, store_i, exit_wave_real, exit_wave_imaginary, in_r, in_i = carry
        slot = tick - section
        valid = (slot >= 0) & (slot < groups)
        start = jnp.clip(slot, 0, groups - 1) * size
        src_r = jnp.where(section == 0, lead_r, in_r)
        src_i = jnp.where(section == 0, lead_i, in_i)
        waves_r, waves_i, output_real, output_imaginary = forward_pass(
            src_r, src_i, pat_r, pat_i, kr, ki
        )
        store_r = place(store_r, waves_r, start, valid)
        store_i = place(store_i, waves_i, start, valid)
        exit_wave_real = place(exit_wave_real, output_real, start, valid)
        exit_wave_imaginary = place(exit_wave_imaginary, output_imaginary, start, valid)
        in_r, in_i = shifted((output_real, output_imaginary), "slab", 1)
        return (store_r, store_i, exit_wave_real, exit_wave_imaginary, in_r, in_i)

    store_r, store_i, exit_wave_real, exit_wave_imaginary, _, _ = lax.fori_loop(
        0, ticks, forward_tick, (stored, stored, exits, exits, field, field)
    )
    chi_all_r, chi_all_i = target_amplitude(
        exit_wave_real, exit_wave_imaginary, intensity, wave_real, wave_imaginary
    )
    plane = jnp.zeros((depth, 2 * width, cols_all), jnp.float32)

    def backward_tick(tick, carry):
        acc_r, acc_i, in_r, in_i = carry
        slot = tick - (nslab - 1 - section)
        valid = (slot >= 0) & (slot < groups)
        start = jnp.clip(slot, 0, groups - 1) * size
        last = section == nslab - 1
        src_r = jnp.where(last, chi_all_r, in_r)
        src_i = jnp.where(last, chi_all_i, in_i)
        chirp_real, chirp_imaginary, term_r, term_i = backward_pass(
            src_r, src_i, store_r, store_i, pat_r, pat_i, kr, ki
        )
        weight = valid.astype(jnp.float32)
        acc_r, acc_i = deposit(acc_r, acc_i, term_r * weight, term_i * weight, row_off, col_off)
        in_r, in_i = shifted((chirp_real, chirp_imaginary), "slab", -1)
        return (acc_r, acc_i, in_r, in_i)

    acc_r, acc_i, _, _ = lax.fori_loop(0, ticks, backward_tick, (plane, plane, field, field))
    rim_r, rim_i = from_behind((acc_r[:, width:], acc_i[:, width:]), "pos", 1)
    return (acc_r[:, :width] + rim_r, acc_i[:, :width] + rim_i)


def solution(mesh):
    in_specs = (
        P(("parts", "slab"), "pos", None),
        P(("parts", "slab"), "pos", None),
        P(),
        P(),
        P(("parts", "pos"), None, None),
        P(("parts", "pos")),
        P(("parts", "pos")),
    )
    out_specs = (P(("parts", "slab"), "pos", None), P(("parts", "slab"), "pos", None))
    return jax.shard_map(local, mesh=mesh, in_specs=in_specs, out_specs=out_specs, check_vma=False)
```

profile of v0, /device:TPU:1, one launch (start us, length us, event | category | flops | bytes accessed | tf_op | source)
XLA Modules:
  0.0 1154.5 jit_solution(10633901247342315576)
XLA Ops:
  0.6 5.2 collective-permute-start.4
  8.4 389.4 %gather_fusion.1 = f32[65536]{0:T(1024)S(1)} fusion(f32[63]{0:T(128)S(1)} %get-tuple-element.1117, s32[65536]{0:T(1024)S(1)} %broadcast_clamp_fusion), kind=kCustom, calls=%fused_computation.1 | custom fusion | bytes 786432 | tf_op jit(solution)/shard_map/gather | solution.py:38
  397.8 389.4 %gather_fusion = f32[65536]{0:T(1024)S(1)} fusion(f32[63]{0:T(128)S(1)} %get-tuple-element.1118, s32[65536]{0:T(1024)S(1)} %broadcast_clamp_fusion), kind=kCustom, calls=%fused_computation | custom fusion | bytes 786432 | tf_op jit(solution)/shard_map/gather | solution.py:38
  787.5 4.8 pad_maximum_fusion
  793.4 7.9 while.81
  794.0 3.4 bitcast_dynamic-update-slice_fusion.4
  798.0 3.3 bitcast_dynamic-update-slice_fusion.4
  801.4 4.8 pad_maximum_fusion.1
  807.2 7.9 while.82
  807.8 3.4 bitcast_dynamic-update-slice_fusion.5
  811.8 3.3 bitcast_dynamic-update-slice_fusion.5
  815.2 59.6 %while.83 = (s32[]{:T(128)}, f32[2,2,256,256]{3,2,0,1:T(8,128)}, f32[2,2,256,256]{3,2,0,1:T(8,128)}, f32[2,256,256]{2,1,0:T(8,128)}, f32[2,256,256]{2,1,0:T(8,12...) while((s32[]{:T(128)}, f32[2,2,256,256]{3,2,0,1:T(8,128)}, ...), condition=%wide.region_1.2_spmd.clone, body=%wide.region_0.1_spmd.clone.sunk | while | flops 6447431680 | bytes 45089048 | solution.py:177
  824.8 3.0 fusion.415
  861.0 3.1 select_select_fusion.4
  866.4 3.0 select_select_fusion.5
  870.7 3.6 maximum_select_fusion.3
  915.9 141.5 %while.80 = (s32[]{:T(128)}, f32[2,512,1024]{2,1,0:T(8,128)}, f32[2,512,1024]{2,1,0:T(8,128)}, f32[2,256,256]{2,1,0:T(8,128)}, f32[2,256,256]{2,1,0:T(8,128)}, /...) while((s32[]{:T(128)}, f32[2,512,1024]{2,1,0:T(8,128)}, ...), condition=%wide.region_5.6_spmd, body=%wide.region_2.5_spmd.sunk | while | flops 6448480256 | bytes 50856612 | solution.py:201
  934.6 4.5 fusion.376
  939.1 6.1 collective-permute-start.2
  949.8 38.8 %while.84 = (s32[]{:T(128)}, f32[2,512,1024]{2,1,0:T(8,128)}, f32[2,512,1024]{2,1,0:T(8,128)}, s32[2]{0:T(128)S(1)}, s32[2]{0:T(128)S(1)}, /*index=5*/f32[2,2,25...) while((s32[]{:T(128)}, f32[2,512,1024]{2,1,0:T(8,128)}, ...), condition=%wide.region_4.4_spmd, body=%wide.region_3.3_spmd.sunk | while | flops 262152 | bytes 5243109 | solution.py:130
  956.1 6.7 dynamic_update_slice.28
  962.8 6.7 dynamic_update_slice.29
  975.8 6.4 dynamic_update_slice.28
  982.2 6.3 dynamic_update_slice.29
  1007.1 4.5 fusion.376
  1018.7 38.8 %while.84 = (s32[]{:T(128)}, f32[2,512,1024]{2,1,0:T(8,128)}, f32[2,512,1024]{2,1,0:T(8,128)}, s32[2]{0:T(128)S(1)}, s32[2]{0:T(128)S(1)}, /*index=5*/f32[2,2,25...) while((s32[]{:T(128)}, f32[2,512,1024]{2,1,0:T(8,128)}, ...), condition=%wide.region_4.4_spmd, body=%wide.region_3.3_spmd.sunk | while | flops 262152 | bytes 5243109 | solution.py:130
  1025.0 6.7 dynamic_update_slice.28
  1031.7 6.7 dynamic_update_slice.29
  1044.7 6.4 dynamic_update_slice.28
  1051.1 6.3 dynamic_update_slice.29
  1062.5 47.3 %collective-permute-done.6 = f32[2,256,1024]{2,1,0:T(8,128)S(1)} collective-permute-done((f32[2,256,1024]{2,1,0:T(8,128)S(1)}, f32[2,256,1024]{2,1,0:T(8,128)S(1)}, u32[]{:S(2)}, u32[]{:S(2)}) %collective-permute-start.6) | collective-permute-done | bytes 2097184 | tf_op jit(solution)/shard_map/ppermute | solution.py:14
  1111.5 41.1 %collective-permute-done.7 = f32[2,256,1024]{2,1,0:T(8,128)S(1)} collective-permute-done((f32[2,256,1024]{2,1,0:T(8,128)S(1)}, f32[2,256,1024]{2,1,0:T(8,128)S(1)}, u32[]{:S(2)}, u32[]{:S(2)}) %collective-permute-start.7) | collective-permute-done | bytes 2097184 | tf_op jit(solution)/shard_map/ppermute | solution.py:14
  (164 shorter events, 163.4 us)
Async XLA Ops:
  0.6 786.9 %collective-permute-start.4 = (f32[2,256,1024]{2,1,0:T(8,128)}, f32[2,256,1024]{2,1,0:T(8,128)}, u32[]{:S(2)}, u32[]{:S(2)}) collective-permute-start(f32[2,256,1024]{2,1,0:T(8,128)} %param.13), channel_id=1, source_target_pairs={{2,0},{4,2},{6,4},{8,6},{10,8},{12,10},{14,12},{0,14},{3,1},{5,3},... | collective-permute-start | bytes 6291464 | tf_op jit(solution)/shard_map/ppermute | solution.py:14
  5.8 795.6 %collective-permute-start.5 = (f32[2,256,1024]{2,1,0:T(8,128)}, f32[2,256,1024]{2,1,0:T(8,128)}, u32[]{:S(2)}, u32[]{:S(2)}) collective-permute-start(f32[2,256,1024]{2,1,0:T(8,128)} %param.14), channel_id=1, source_target_pairs={{2,0},{4,2},{6,4},{8,6},{10,8},{12,10},{14,12},{0,14},{3,1},{5,3},... | collective-permute-start | bytes 6291464 | tf_op jit(solution)/shard_map/ppermute | solution.py:14
  397.8 389.6 %copy-start.4 = (f32[2,256,256]{2,1,0:T(8,128)S(1)}, f32[2,256,256]{2,1,0:T(8,128)}, u32[]{:S(2)}) copy-start(f32[2,256,256]{2,1,0:T(8,128)} %param.15) | copy-start | bytes 1572868
  787.5 5.9 copy-start.5
  834.9 8.5 collective-permute-start
  839.2 4.2 collective-permute-start.1
  864.1 10.2 collective-permute-start
  869.5 4.9 collective-permute-start.1
  874.8 12.4 %copy-start.2 = (f32[2,256,256]{2,1,0:T(8,128)S(1)}, f32[2,256,256]{2,1,0:T(8,128)}, u32[]{:S(2)}) copy-start(f32[2,256,256]{2,1,0:T(8,128)} %get-tuple-element.813) | copy-start | bytes 1572868
  880.5 12.4 %copy-start.3 = (f32[2,256,256]{2,1,0:T(8,128)S(1)}, f32[2,256,256]{2,1,0:T(8,128)}, u32[]{:S(2)}) copy-start(f32[2,256,256]{2,1,0:T(8,128)} %param.17) | copy-start | bytes 1572868
  910.9 5.0 copy-start.6
  910.9 5.0 copy-start.7
  939.1 49.4 %collective-permute-start.2 = (f32[2,256,256]{2,1,0:T(8,128)}, f32[2,256,256]{2,1,0:T(8,128)}, u32[]{:S(2)}, u32[]{:S(2)}) collective-permute-start(f32[2,256,256]{2,1,0:T(8,128)} %get-tuple-element.1436), channel_id=1, source_target_pairs={{1,0},{3,2},{5,4},{7,6},{9,8},{11,10},{13,12},{15,14},{17,16},{19,... | collective-permute-start | bytes 1572872 | tf_op jit(solution)/shard_map/while/body/eval_jaxpr/ppermute | solution.py:20
  945.2 43.3 %collective-permute-start.3 = (f32[2,256,256]{2,1,0:T(8,128)}, f32[2,256,256]{2,1,0:T(8,128)}, u32[]{:S(2)}, u32[]{:S(2)}) collective-permute-start(f32[2,256,256]{2,1,0:T(8,128)} %get-tuple-element.1437), channel_id=1, source_target_pairs={{1,0},{3,2},{5,4},{7,6},{9,8},{11,10},{13,12},{15,14},{17,16},{19,... | collective-permute-start | bytes 1572872 | tf_op jit(solution)/shard_map/while/body/eval_jaxpr/ppermute | solution.py:20
  1011.6 45.9 %collective-permute-start.2 = (f32[2,256,256]{2,1,0:T(8,128)}, f32[2,256,256]{2,1,0:T(8,128)}, u32[]{:S(2)}, u32[]{:S(2)}) collective-permute-start(f32[2,256,256]{2,1,0:T(8,128)} %get-tuple-element.1436), channel_id=1, source_target_pairs={{1,0},{3,2},{5,4},{7,6},{9,8},{11,10},{13,12},{15,14},{17,16},{19,... | collective-permute-start | bytes 1572872 | tf_op jit(solution)/shard_map/while/body/eval_jaxpr/ppermute | solution.py:20
  1014.1 43.3 %collective-permute-start.3 = (f32[2,256,256]{2,1,0:T(8,128)}, f32[2,256,256]{2,1,0:T(8,128)}, u32[]{:S(2)}, u32[]{:S(2)}) collective-permute-start(f32[2,256,256]{2,1,0:T(8,128)} %get-tuple-element.1437), channel_id=1, source_target_pairs={{1,0},{3,2},{5,4},{7,6},{9,8},{11,10},{13,12},{15,14},{17,16},{19,... | collective-permute-start | bytes 1572872 | tf_op jit(solution)/shard_map/while/body/eval_jaxpr/ppermute | solution.py:20
  1057.5 3.9 copy-start
  1057.5 52.4 %copy-start.1 = (f32[2,512,1024]{2,1,0:T(8,128)S(1)}, f32[2,512,1024]{2,1,0:T(8,128)}, u32[]{:S(2)}) copy-start(f32[2,512,1024]{2,1,0:T(8,128)} %get-tuple-element.1707) | copy-start | bytes 12582916
  1059.4 50.5 %collective-permute-start.6 = (f32[2,256,1024]{2,1,0:T(8,128)S(1)}, f32[2,256,1024]{2,1,0:T(8,128)S(1)}, u32[]{:S(2)}, u32[]{:S(2)}) collective-permute-start(f32[2,256,1024]{2,1,0:T(8,128)S(1)} %slice.133), channel_id=1, source_target_pairs={{14,0},{0,2},{2,4},{4,6},{6,8},{8,10},{10,12},{12,14},{15,1},{1,3}... | collective-permute-start | bytes 6291464 | tf_op jit(solution)/shard_map/ppermute | solution.py:14
  1061.6 91.1 %collective-permute-start.7 = (f32[2,256,1024]{2,1,0:T(8,128)S(1)}, f32[2,256,1024]{2,1,0:T(8,128)S(1)}, u32[]{:S(2)}, u32[]{:S(2)}) collective-permute-start(f32[2,256,1024]{2,1,0:T(8,128)S(1)} %slice.135), channel_id=1, source_target_pairs={{14,0},{0,2},{2,4},{4,6},{6,8},{8,10},{10,12},{12,14},{15,1},{1,3}... | collective-permute-start | bytes 6291464 | tf_op jit(solution)/shard_map/ppermute | solution.py:14
where the time goes:
time: 1160 us; the launch traced here: 1150 us
  local copies, waits for them, and re-layouts  864 us (74%)
  matrix products  122 us (11%)
  waiting for transfers between devices  88.5 us (8%)
  other arithmetic  37.7 us (3%)
  starting transfers between devices  26.3 us (2%)
  loops' own time  14.5 us (1%)
    gather x2, local copies, waits for them, and re-layouts, band(): taps[0][index]  389 us
    gather x2, local copies, waits for them, and re-layouts, band(): taps[1][index]  389 us
    dot_general x80, matrix products, mul(): jnp.einsum(form, left, right, precision=HIGH, preferred_element_type=jnp....  122 us
    ppermute x4, waiting for transfers between devices, from_behind(): return lax.ppermute(block, axis, route)  88.5 us
    dynamic_update_slice x4, local copies, waits for them, and re-layouts, add_one(): total_r = lax.dynamic_update_slice(total_r, now_r + term_r[item], start)  26.1 us
    dynamic_update_slice x4, local copies, waits for them, and re-layouts, add_one(): total_i = lax.dynamic_update_slice(total_i, now_i + term_i[item], start)  26.1 us
  transfers between devices with their start and end apart: 12, of which 2 were waited for; matrix products, arithmetic and copies ran while one was open for 76% of the time, Pallas kernels for 0%

commit v1 on v0

v1 whole, which is shorter than its diff:
```python
import math

import jax
import jax.numpy as jnp
import numpy as np
from jax import lax
from jax.experimental import pallas as pl
from jax.experimental.pallas import tpu as pltpu
from jax.sharding import PartitionSpec as P

F32 = jnp.float32
BF16 = jnp.bfloat16
SMEM = pl.BlockSpec(memory_space=pltpu.SMEM)
VMEM = pl.BlockSpec(memory_space=pltpu.VMEM)


def halves(x):
    high = x.astype(BF16)
    return high, (x - high.astype(F32)).astype(BF16)


def left_mul(high, low, x):
    xh, xl = halves(x)
    left = jnp.concatenate([high, high, low], 1)
    right = jnp.concatenate([xh, xl, xh], 0)
    return jnp.dot(left, right, preferred_element_type=F32)


def right_mul(x, high, low):
    xh, xl = halves(x)
    left = jnp.concatenate([xh, xl, xh], 1)
    right = jnp.concatenate([high, high, low], 0)
    return jnp.dot(left, right, preferred_element_type=F32)


def sandwich(left_h, left_l, xr, xi, right_h, right_l):
    n = xr.shape[0]
    y = left_mul(left_h, left_l, jnp.concatenate([xr, xi], 0))
    z = right_mul(jnp.concatenate([y[:n], y[n:]], 1), right_h, right_l)
    return z[:, :n], z[:, n:]


def fourier_blocks(n):
    steps = np.arange(n)
    angle = 2.0 * math.pi / n * ((steps[:, None] * steps[None, :]) % n)
    norm = 1.0 / math.sqrt(n)
    wr, wi = np.cos(angle) * norm, -np.sin(angle) * norm
    c = np.block([[wr, -wi], [wi, wr]]).astype(np.float32)
    d = np.block([[wr, wi], [-wi, wr]]).astype(np.float32)
    out = []
    for m in (c, d):
        high = m.astype(jnp.bfloat16)
        out += [high, (m - high.astype(np.float32)).astype(jnp.bfloat16)]
    return [jnp.asarray(m) for m in out]


def column_place(col, cols_all, span):
    base = jnp.minimum(col // 128 * 128, cols_all - span)
    return pl.multiple_of(base, 128), col - base


def cut_kernel(cols, obj_r, obj_i, own_s, own_o, halo_s, halo_o):
    n = own_s.shape[-1]
    span = n + 128
    for k, out in enumerate((own_s, own_o, halo_s, halo_o)):
        base, shift = column_place(cols[k], obj_r.shape[-1], span)
        for ri, src in enumerate((obj_r, obj_i)):
            wide = src[0, :, pl.ds(base, span)]
            out[ri, 0] = pltpu.roll(wide, lax.rem(span - shift, span), 1)[:, :n]


def wave_kernel(
    info, own_s, own_o, halo_s, halo_o, probe, ring, intensity, ch, cl, dh, dl,
    term_s, term_o, patch, waves, ah, al, bh, bl,
):
    n = probe.shape[-1]
    depth = own_s.shape[1]
    section, row = info[0], info[1]
    unroll_by = lax.rem(n - row, n)
    from_next = lax.broadcasted_iota(jnp.int32, (n, n), 0) < row
    for own, halo, where in ((own_s, halo_s, section), (own_o, halo_o, 1 - section)):
        for d in range(depth):
            for ri in range(2):
                merged = jnp.where(from_next, halo[ri, d], own[ri, d])
                patch[where * depth + d, ri] = pltpu.roll(merged, unroll_by, 0)

    def toeplitz(k):
        rows = jnp.broadcast_to(ring[k : k + 1, :], (n, 2 * n))
        return pltpu.roll(rows, 0, 1, stride=1, stride_axis=0)[:, :n]

    for high, low, kr, ki in ((ah, al, toeplitz(0), -toeplitz(1)), (bh, bl, toeplitz(2), toeplitz(3))):
        for r0, c0, block in ((0, 0, kr), (0, n, ki), (n, 0, -ki), (n, n, kr)):
            hi, lo = halves(block)
            high[r0 : r0 + n, c0 : c0 + n] = hi
            low[r0 : r0 + n, c0 : c0 + n] = lo

    waves[0] = probe[...]
    slices = 2 * depth

    def forward(s, _):
        pr, pi = waves[s, 0], waves[s, 1]
        o_r, o_i = patch[s, 0], patch[s, 1]
        zr, zi = sandwich(
            ah[...], al[...], pr * o_r - pi * o_i, pr * o_i + pi * o_r, bh[...], bl[...]
        )
        waves[s + 1, 0] = zr
        waves[s + 1, 1] = zi
        return 0

    lax.fori_loop(0, slices, forward, 0)
    fr, fi = sandwich(
        ch[...], cl[...], waves[slices, 0], waves[slices, 1], dh[...], dl[...]
    )
    residual = 2.0 * (fr * fr + fi * fi - intensity[section])
    xr, xi = sandwich(dh[...], dl[...], residual * fr, residual * fi, ch[...], cl[...])
    waves[slices, 0] = xr
    waves[slices, 1] = xi

    def backward(t, _):
        s = slices - 1 - t
        a_r, a_i = sandwich(
            bh[...], bl[...], waves[s + 1, 0], waves[s + 1, 1], ah[...], al[...]
        )
        w_r, w_i = waves[s, 0], waves[s, 1]
        o_r, o_i = patch[s, 0], patch[s, 1]
        patch[s, 0] = a_r * w_r + a_i * w_i
        patch[s, 1] = a_i * w_r - a_r * w_i
        waves[s, 0] = a_r * o_r + a_i * o_i
        waves[s, 1] = a_i * o_r - a_r * o_i
        return 0

    lax.fori_loop(0, slices, backward, 0)
    for out, where in ((term_s, section), (term_o, 1 - section)):
        for d in range(depth):
            for ri in range(2):
                out[ri, d] = pltpu.roll(patch[where * depth + d, ri], row, 0)


def deposit_kernel(rows, cols, own_s, own_o, rim_s, rim_o, out_r, out_i):
    n = own_s.shape[-1]
    span = n + 128
    row_index = lax.broadcasted_iota(jnp.int32, (n, n), 0)
    for ri, out in enumerate((out_r, out_i)):
        out[...] = jnp.zeros_like(out)
        for k, src in enumerate((own_s, own_o, rim_s, rim_o)):
            keep = row_index >= rows[k] if k < 2 else row_index < rows[k]
            term = jnp.where(keep, src[ri, 0], 0.0)
            base, shift = column_place(cols[k], out.shape[-1], span)
            wide = jnp.concatenate([term, jnp.zeros((n, 128), F32)], 1)
            out[0, :, pl.ds(base, span)] += pltpu.roll(wide, shift, 1)


def local(obj_real, obj_imag, probe, taps, intensity, row_off, col_off):
    n = probe.shape[-1]
    depth, tile, cols_all = obj_real.shape
    npos, nslab = lax.axis_size("pos"), lax.axis_size("slab")
    section = lax.axis_index("slab")

    def ring_pairs(step, flip):
        pairs = []
        for p in range(npos):
            for s in range(nslab):
                to = ((p + step) % npos) * nslab + (1 - s if flip else s)
                pairs.append((p * nslab + s, to))
        return pairs

    def send(x, step, flip):
        return lax.ppermute(x, ("pos", "slab"), ring_pairs(step, flip))

    order = jnp.stack([section, 1 - section])
    mine = jnp.stack([row_off, col_off])[:, order]
    before = send(mine, 1, False)
    rows = jnp.concatenate([mine[0], before[0]])
    cols = jnp.concatenate([mine[1], before[1]])

    window = jax.ShapeDtypeStruct((2, depth, n, n), F32)
    window_spec = pl.BlockSpec((2, 1, n, n), lambda d: (0, d, 0, 0))
    plane_spec = pl.BlockSpec((1, tile, cols_all), lambda d: (d, 0, 0))
    own_s, own_o, halo_s, halo_o = pl.pallas_call(
        cut_kernel,
        grid=(depth,),
        out_shape=[window] * 4,
        in_specs=[SMEM, plane_spec, plane_spec],
        out_specs=[window_spec] * 4,
        compiler_params=pltpu.CompilerParams(vmem_limit_bytes=40 * 2**20),
        name="cut",
    )(cols, obj_real, obj_imag)
    halo_s = send(halo_s, -1, False)
    halo_o = send(halo_o, -1, True)
    own_o = send(own_o, 0, True)

    half = (taps.shape[1] - 1) // 2
    gap = jnp.zeros((2, 2 * n - taps.shape[1]), F32)
    back = taps[:, ::-1]
    ring = jnp.concatenate(
        [
            jnp.concatenate([t[:, half:], gap, t[:, :half]], 1)
            for t in (taps, back)
        ],
        0,
    )
    info = jnp.stack([section, rows[0]]).astype(jnp.int32)
    square = pltpu.VMEM((2 * n, 2 * n), BF16)
    term_s, term_o = pl.pallas_call(
        wave_kernel,
        out_shape=[window] * 2,
        in_specs=[SMEM] + [VMEM] * 11,
        out_specs=[VMEM] * 2,
        scratch_shapes=[
            pltpu.VMEM((2 * depth, 2, n, n), F32),
            pltpu.VMEM((2 * depth + 1, 2, n, n), F32),
            square, square, square, square,
        ],
        compiler_params=pltpu.CompilerParams(vmem_limit_bytes=48 * 2**20),
        name="waves",
    )(info, own_s, own_o, halo_s, halo_o, probe, ring, intensity, *fourier_blocks(n))

    rim_s = send(term_s, 1, False)
    rim_o = send(term_o, 1, True)
    own_o = send(term_o, 0, True)
    return pl.pallas_call(
        deposit_kernel,
        grid=(depth,),
        out_shape=[jax.ShapeDtypeStruct(obj_real.shape, F32)] * 2,
        in_specs=[SMEM, SMEM] + [window_spec] * 4,
        out_specs=[plane_spec] * 2,
        compiler_params=pltpu.CompilerParams(vmem_limit_bytes=40 * 2**20),
        name="deposit",
    )(rows, cols, term_s, own_o, rim_s, rim_o)


def solution(mesh):
    in_specs = (
        P(("parts", "slab"), "pos", None),
        P(("parts", "slab"), "pos", None),
        P(),
        P(),
        P(("parts", "pos"), None, None),
        P(("parts", "pos")),
        P(("parts", "pos")),
    )
    out_specs = (P(("parts", "slab"), "pos", None), P(("parts", "slab"), "pos", None))
    return jax.shard_map(local, mesh=mesh, in_specs=in_specs, out_specs=out_specs, check_vma=False)
```

time: 1160 us -> 144 us (0.12)
  local copies, waits for them, and re-layouts: 864 us -> 7.49 us
  matrix products: 122 us -> 0 us
  other arithmetic: 37.7 us -> 1.1 us
  Pallas kernels: 0 us -> 30 us
  starting transfers between devices: 26.3 us -> 8.06 us
  loops' own time: 14.5 us -> 0 us
    gather x16 -> x1, local copies, waits for them, and re-layouts: 795 us -> 0.56 us  [local(): mine = jnp.stack([row_off, col_off])[:, order]]
    dot_general x80 -> x0, matrix products: 122 us -> none  [mul(): jnp.einsum(form, left, right, precision=HIGH, preferred_element_type=jnp....]
    dynamic_update_slice x8 -> x0, local copies, waits for them, and re-layouts: 52.2 us -> none  [the longest x4 26.1 us: add_one(): total_r = lax.dynamic_update_slice(total_r, now_r + term_r[item], start)]
    pallas_call x0 -> x3, Pallas kernels: none -> 30 us  [the longest x1 22.1 us: local(): pl.pallas_call(wave_kernel, out_shape=[window] * 2, in_specs=[SMEM] + [VM...]
    ppermute x12 -> x7, starting transfers between devices: 26.3 us -> 8.06 us  [send(): return lax.ppermute(x, ('pos', 'slab'), ring_pairs(step, flip))]
    add x8 -> x0, other arithmetic: 15.9 us -> none  [the longest x4 7.69 us: add_one(): total_i = lax.dynamic_update_slice(total_i, now_i + term_i[item], start)]
    another operation x6 -> x0, loops' own time: 14.5 us -> none  [the longest x2 13.2 us: deposit(): return lax.fori_loop(0, term_r.shape[0], add_one, (acc_r, acc_i))]
    ppermute x12 -> x7, waiting for transfers between devices: 88.5 us -> 95.7 us  [send(): return lax.ppermute(x, ('pos', 'slab'), ring_pairs(step, flip))]
  transfers between devices with their start and end apart: 12 -> 7, of which waited for: 2 -> 5; matrix products, arithmetic and copies ran while one was open for 76% -> 1% of each run, Pallas kernels for 0% -> 0%
where the time goes in v1:
time: 144 us; the launch traced here: 143 us
  waiting for transfers between devices  95.7 us (66%)
  Pallas kernels  30 us (21%)
  starting transfers between devices  8.06 us (6%)
  local copies, waits for them, and re-layouts  7.49 us (5%)
    ppermute x7, waiting for transfers between devices, send(): return lax.ppermute(x, ('pos', 'slab'), ring_pairs(step, flip))  95.7 us
    pallas_call x1, Pallas kernels, local(): pl.pallas_call(wave_kernel, out_shape=[window] * 2, in_specs=[SMEM] + [VM...  22.1 us
    ppermute x7, starting transfers between devices, send(): return lax.ppermute(x, ('pos', 'slab'), ring_pairs(step, flip))  8.06 us
    unnamed x20, local copies, waits for them, and re-layouts  4.22 us
    pallas_call x1, Pallas kernels, local(): pl.pallas_call(deposit_kernel, grid=(depth,), out_shape=[jax.ShapeDtypeSt...  4.19 us
    pallas_call x1, Pallas kernels, local(): pl.pallas_call(cut_kernel, grid=(depth,), out_shape=[window] * 4, in_spec...  3.68 us
  transfers between devices with their start and end apart: 7, of which 5 were waited for; matrix products, arithmetic and copies ran while one was open for 1% of the time, Pallas kernels for 0%

profile of v1, /device:TPU:1, one launch (start us, length us, event | category | flops | bytes accessed | tf_op | source)
XLA Modules:
  0.0 143.1 jit_solution(1599574107653797832)
XLA Ops:
  0.6 0.7 copy.15
  1.4 0.7 copy.16
  2.1 0.1 fusion
  2.2 0.1 pad_add_fusion
  2.3 0.6 gather_fusion
  2.8 2.1 %collective-permute-start = (s32[2,2]{0,1:T(2,128)S(1)}, s32[2,2]{0,1:T(2,128)S(1)}, u32[]{:S(2)}, u32[]{:S(2)}) collective-permute-start(s32[2,2]{0,1:T(2,128)S(1)} %bitcast.9), channel_id=1, source_target_pairs={{0,2},{1,3},{2,4},{3,5},{4,6},{5,7},{6,8},{7,9},{8,10},{9,11},{10,... | collective-permute-start | bytes 56 | tf_op jit(solution)/shard_map/ppermute | solution.py:168
  5.0 0.2 slice_reduce_fusion.1
  5.1 3.8 %collective-permute-done = s32[2,2]{0,1:T(2,128)S(1)} collective-permute-done((s32[2,2]{0,1:T(2,128)S(1)}, s32[2,2]{0,1:T(2,128)S(1)}, u32[]{:S(2)}, u32[]{:S(2)}) %collective-permute-start) | collective-permute-done | bytes 48 | tf_op jit(solution)/shard_map/ppermute | solution.py:168
  9.0 0.2 slice_reduce_fusion
  9.1 0.1 pad_add_fusion.2.cols
  9.2 1.6 %copy-done = f32[2,256,1024]{2,1,0:T(8,128)S(1)} copy-done((f32[2,256,1024]{2,1,0:T(8,128)S(1)}, f32[2,256,1024]{2,1,0:T(8,128)}, u32[]{:S(2)}) %copy-start) | copy-done | bytes 2097176
  10.8 1.6 %copy-done.1 = f32[2,256,1024]{2,1,0:T(8,128)S(1)} copy-done((f32[2,256,1024]{2,1,0:T(8,128)S(1)}, f32[2,256,1024]{2,1,0:T(8,128)}, u32[]{:S(2)}) %copy-start.1) | copy-done | bytes 2097176
  12.4 3.7 %cut.1 = (f32[2,2,256,256]{3,2,1,0:T(8,128)S(1)}, f32[2,2,256,256]{3,2,1,0:T(8,128)}, f32[2,2,256,256]{3,2,1,0:T(8,128)}, f32[2,2,256,256]{3,2,1,0:T(8,128)}) custom-call(s32[4]{0:T(128)S(1)} %pad_add_fusion.2.cols, f32[2,256,1024]{2,1,0:T(8,128)S(1)} %copy-done, f32[2,256,1024]{2,1,0:T(8,128)S(1)} %copy-done.1), custom_call_target="tpu_custom_call" | custom-call | tf_op jit(solution)/shard_map/cut/pallas_call | solution.py:179
  16.1 1.0 copy-done.2
  17.1 1.5 %collective-permute-start.1 = (f32[2,2,256,256]{3,2,1,0:T(8,128)}, f32[2,2,256,256]{3,2,1,0:T(8,128)}, u32[]{:S(2)}, u32[]{:S(2)}) collective-permute-start(f32[2,2,256,256]{3,2,1,0:T(8,128)} %get-tuple-element.9), channel_id=1, source_target_pairs={{0,1},{1,0},{2,3},{3,2},{4,5},{5,4},{6,7},{7,6},{8,9},{9,8},{10,11... | collective-permute-start | bytes 3145736 | tf_op jit(solution)/shard_map/ppermute | solution.py:168
  18.7 1.7 %collective-permute-start.2 = (f32[2,2,256,256]{3,2,1,0:T(8,128)}, f32[2,2,256,256]{3,2,1,0:T(8,128)}, u32[]{:S(2)}, u32[]{:S(2)}) collective-permute-start(f32[2,2,256,256]{3,2,1,0:T(8,128)} %get-tuple-element.10), channel_id=1, source_target_pairs={{0,14},{1,15},{2,0},{3,1},{4,2},{5,3},{6,4},{7,5},{8,6},{9,7},{10,... | collective-permute-start | bytes 3145736 | tf_op jit(solution)/shard_map/ppermute | solution.py:168
  20.4 1.3 collective-permute-start.3
  21.7 0.5 slice.41
  22.2 0.1 fusion.2
  22.3 0.1 slice.48
  22.4 0.1 fusion.1
  22.5 0.1 slice.46
  22.6 0.7 pad_add_fusion.3.info
  23.3 0.1 maximum_maximum_fusion.ring
  23.4 20.4 %collective-permute-done.2.halo_s = f32[2,2,256,256]{3,2,1,0:T(8,128)} collective-permute-done((f32[2,2,256,256]{3,2,1,0:T(8,128)}, f32[2,2,256,256]{3,2,1,0:T(8,128)}, u32[]{:S(2)}, u32[]{:S(2)}) %collective-permute-start.2) | collective-permute-done | bytes 1048608 | tf_op jit(solution)/shard_map/ppermute | solution.py:168
  43.8 22.6 %collective-permute-done.3.halo_o = f32[2,2,256,256]{3,2,1,0:T(8,128)} collective-permute-done((f32[2,2,256,256]{3,2,1,0:T(8,128)}, f32[2,2,256,256]{3,2,1,0:T(8,128)}, u32[]{:S(2)}, u32[]{:S(2)}) %collective-permute-start.3) | collective-permute-done | bytes 1048608 | tf_op jit(solution)/shard_map/ppermute | solution.py:168
  66.4 22.1 %waves.1 = (f32[2,2,256,256]{3,2,1,0:T(8,128)S(1)}, f32[2,2,256,256]{3,2,1,0:T(8,128)S(1)}) custom-call(s32[2]{0:T(128)S(1)} %pad_add_fusion.3.info, f32[2,2,256,256]{3,2,1,0:T(8,128)} %copy-done.2, f32[2,2,256,256]{3,2,1,0:T(8,128)} %collective-permute-done.1.own_o, f32[2,2,256,256]{3,2,1,0:T(8,128)} %collective-permute-done.2.halo_s, ...), custom_call_target="tpu_custom_call" | custom-call | tf_op jit(solution)/shard_map/waves/pallas_call | solution.py:204
  88.5 1.3 collective-permute-start.6
  89.8 0.1 pad_add_fusion.1.rows
  89.9 26.4 %collective-permute-done.5.rim_s = f32[2,2,256,256]{3,2,1,0:T(8,128)S(1)} collective-permute-done((f32[2,2,256,256]{3,2,1,0:T(8,128)S(1)}, f32[2,2,256,256]{3,2,1,0:T(8,128)S(1)}, u32[]{:S(2)}, u32[]{:S(2)}) %collective-permute-start.5) | collective-permute-done | bytes 1048608 | tf_op jit(solution)/shard_map/ppermute | solution.py:168
  116.3 22.6 %collective-permute-done.6.rim_o = f32[2,2,256,256]{3,2,1,0:T(8,128)S(1)} collective-permute-done((f32[2,2,256,256]{3,2,1,0:T(8,128)S(1)}, f32[2,2,256,256]{3,2,1,0:T(8,128)S(1)}, u32[]{:S(2)}, u32[]{:S(2)}) %collective-permute-start.6) | collective-permute-done | bytes 1048608 | tf_op jit(solution)/shard_map/ppermute | solution.py:168
  138.9 4.2 %deposit.1 = (f32[2,256,1024]{2,1,0:T(8,128)}, f32[2,256,1024]{2,1,0:T(8,128)}) custom-call(s32[4]{0:T(128)S(1)} %pad_add_fusion.1.rows, s32[4]{0:T(128)S(1)} %pad_add_fusion.2.cols, f32[2,2,256,256]{3,2,1,0:T(8,128)S(1)} %get-tuple-element.12.own_s, f32[2,2,256,256]{3,2,1,0:T(8,128)S(1)} %collective-permute-done.4.own_o, ...), custom_call_target="tpu_custom_call" | custom-call | tf_op jit(solution)/shard_map/deposit/pallas_call | solution.py:221
  (23 shorter events, 0.1 us)
Async XLA Ops:
  2.8 6.1 %collective-permute-start = (s32[2,2]{0,1:T(2,128)S(1)}, s32[2,2]{0,1:T(2,128)S(1)}, u32[]{:S(2)}, u32[]{:S(2)}) collective-permute-start(s32[2,2]{0,1:T(2,128)S(1)} %bitcast.9), channel_id=1, source_target_pairs={{0,2},{1,3},{2,4},{3,5},{4,6},{5,7},{6,8},{7,9},{8,10},{9,11},{10,... | collective-permute-start | bytes 56 | tf_op jit(solution)/shard_map/ppermute | solution.py:168
  9.2 1.6 %copy-start = (f32[2,256,1024]{2,1,0:T(8,128)S(1)}, f32[2,256,1024]{2,1,0:T(8,128)}, u32[]{:S(2)}) copy-start(f32[2,256,1024]{2,1,0:T(8,128)} %obj_r.1) | copy-start | bytes 6291460
  10.8 1.6 %copy-start.1 = (f32[2,256,1024]{2,1,0:T(8,128)S(1)}, f32[2,256,1024]{2,1,0:T(8,128)}, u32[]{:S(2)}) copy-start(f32[2,256,1024]{2,1,0:T(8,128)} %obj_i.1) | copy-start | bytes 6291460
  12.4 9.9 %copy-start.9 = (f32[2,63]{1,0:T(2,128)S(1)}, f32[2,63]{1,0:T(2,128)}, u32[]{:S(2)}) copy-start(f32[2,63]{1,0:T(2,128)} %param.14) | copy-start | bytes 1516
  12.4 53.9 %copy-start.3 = (f32[2,256,256]{2,1,0:T(8,128)S(1)}, f32[2,256,256]{2,1,0:T(8,128)}, u32[]{:S(2)}) copy-start(f32[2,256,256]{2,1,0:T(8,128)} %probe.1) | copy-start | bytes 1572868
  12.4 53.9 %copy-start.4 = (f32[2,256,256]{2,1,0:T(8,128)S(1)}, f32[2,256,256]{2,1,0:T(8,128)}, u32[]{:S(2)}) copy-start(f32[2,256,256]{2,1,0:T(8,128)} %intensity.1) | copy-start | bytes 1572868
  12.4 53.9 %copy-start.5 = (bf16[512,512]{1,0:T(8,128)(2,1)S(1)}, bf16[512,512]{1,0:T(8,128)(2,1)}, u32[]{:S(2)}) copy-start(bf16[512,512]{1,0:T(8,128)(2,1)} %constant.23.clone.dl) | copy-start | bytes 1572868
  12.4 53.9 %copy-start.6 = (bf16[512,512]{1,0:T(8,128)(2,1)S(1)}, bf16[512,512]{1,0:T(8,128)(2,1)}, u32[]{:S(2)}) copy-start(bf16[512,512]{1,0:T(8,128)(2,1)} %constant.22.clone.dh) | copy-start | bytes 1572868
  12.4 53.9 %copy-start.7 = (bf16[512,512]{1,0:T(8,128)(2,1)S(1)}, bf16[512,512]{1,0:T(8,128)(2,1)}, u32[]{:S(2)}) copy-start(bf16[512,512]{1,0:T(8,128)(2,1)} %constant.21.clone.cl) | copy-start | bytes 1572868
  12.4 53.9 %copy-start.8 = (bf16[512,512]{1,0:T(8,128)(2,1)S(1)}, bf16[512,512]{1,0:T(8,128)(2,1)}, u32[]{:S(2)}) copy-start(bf16[512,512]{1,0:T(8,128)(2,1)} %constant.20.clone.ch) | copy-start | bytes 1572868
  16.1 1.0 copy-start.2
  17.1 6.3 %collective-permute-start.1 = (f32[2,2,256,256]{3,2,1,0:T(8,128)}, f32[2,2,256,256]{3,2,1,0:T(8,128)}, u32[]{:S(2)}, u32[]{:S(2)}) collective-permute-start(f32[2,2,256,256]{3,2,1,0:T(8,128)} %get-tuple-element.9), channel_id=1, source_target_pairs={{0,1},{1,0},{2,3},{3,2},{4,5},{5,4},{6,7},{7,6},{8,9},{9,8},{10,11... | collective-permute-start | bytes 3145736 | tf_op jit(solution)/shard_map/ppermute | solution.py:168
  18.7 25.1 %collective-permute-start.2 = (f32[2,2,256,256]{3,2,1,0:T(8,128)}, f32[2,2,256,256]{3,2,1,0:T(8,128)}, u32[]{:S(2)}, u32[]{:S(2)}) collective-permute-start(f32[2,2,256,256]{3,2,1,0:T(8,128)} %get-tuple-element.10), channel_id=1, source_target_pairs={{0,14},{1,15},{2,0},{3,1},{4,2},{5,3},{6,4},{7,5},{8,6},{9,7},{10,... | collective-permute-start | bytes 3145736 | tf_op jit(solution)/shard_map/ppermute | solution.py:168
  20.4 45.9 %collective-permute-start.3 = (f32[2,2,256,256]{3,2,1,0:T(8,128)}, f32[2,2,256,256]{3,2,1,0:T(8,128)}, u32[]{:S(2)}, u32[]{:S(2)}) collective-permute-start(f32[2,2,256,256]{3,2,1,0:T(8,128)} %get-tuple-element.11), channel_id=1, source_target_pairs={{0,15},{1,14},{2,1},{3,0},{4,3},{5,2},{6,5},{7,4},{8,7},{9,6},{10,... | collective-permute-start | bytes 3145736 | tf_op jit(solution)/shard_map/ppermute | solution.py:168
  88.5 27.8 %collective-permute-start.5 = (f32[2,2,256,256]{3,2,1,0:T(8,128)S(1)}, f32[2,2,256,256]{3,2,1,0:T(8,128)S(1)}, u32[]{:S(2)}, u32[]{:S(2)}) collective-permute-start(f32[2,2,256,256]{3,2,1,0:T(8,128)S(1)} %get-tuple-element.12.own_s), channel_id=1, source_target_pairs={{0,2},{1,3},{2,4},{3,5},{4,6},{5,7},{6,8},{7,9},{8,10},{9,11},{10,... | collective-permute-start | bytes 3145736 | tf_op jit(solution)/shard_map/ppermute | solution.py:168
  88.5 50.3 %collective-permute-start.6 = (f32[2,2,256,256]{3,2,1,0:T(8,128)S(1)}, f32[2,2,256,256]{3,2,1,0:T(8,128)S(1)}, u32[]{:S(2)}, u32[]{:S(2)}) collective-permute-start(f32[2,2,256,256]{3,2,1,0:T(8,128)S(1)} %get-tuple-element.13), channel_id=1, source_target_pairs={{0,3},{1,2},{2,5},{3,4},{4,7},{5,6},{6,9},{7,8},{8,11},{9,10},{10,... | collective-permute-start | bytes 3145736 | tf_op jit(solution)/shard_map/ppermute | solution.py:168
  89.8 49.0 %collective-permute-start.4 = (f32[2,2,256,256]{3,2,1,0:T(8,128)S(1)}, f32[2,2,256,256]{3,2,1,0:T(8,128)S(1)}, u32[]{:S(2)}, u32[]{:S(2)}) collective-permute-start(f32[2,2,256,256]{3,2,1,0:T(8,128)S(1)} %get-tuple-element.13), channel_id=1, source_target_pairs={{0,1},{1,0},{2,3},{3,2},{4,5},{5,4},{6,7},{7,6},{8,9},{9,8},{10,11... | collective-permute-start | bytes 3145736 | tf_op jit(solution)/shard_map/ppermute | solution.py:168

commit v2 on v1

--- a/solution.py
+++ b/solution.py
@@ -1,3 +1,4 @@
+import functools
 import math
 
 import jax
@@ -59,17 +60,27 @@
     return pl.multiple_of(base, 128), col - base
 
 
-def cut_kernel(cols, obj_r, obj_i, own_s, own_o, halo_s, halo_o):
-    n = own_s.shape[-1]
+def cut_kernel(cols, obj_r, obj_i, *rest):
+    outs = rest[-cols.shape[0] :]
+    n = outs[0].shape[-1]
     span = n + 128
-    for k, out in enumerate((own_s, own_o, halo_s, halo_o)):
+    for k, out in enumerate(outs):
         base, shift = column_place(cols[k], obj_r.shape[-1], span)
         for ri, src in enumerate((obj_r, obj_i)):
             wide = src[0, :, pl.ds(base, span)]
             out[ri, 0] = pltpu.roll(wide, lax.rem(span - shift, span), 1)[:, :n]
 
 
-def wave_kernel(
+def wave_kernel(phase, info, *refs):
+    if phase > 0:
+        refs = refs[:11] + refs[12:]
+
+    @pl.when(info[0] == phase)
+    def _():
+        wave_body(info, *refs)
+
+
+def wave_body(
     info, own_s, own_o, halo_s, halo_o, probe, ring, intensity, ch, cl, dh, dl,
     term_s, term_o, patch, waves, ah, al, bh, bl,
 ):
@@ -136,15 +147,18 @@
                 out[ri, d] = pltpu.roll(patch[where * depth + d, ri], row, 0)
 
 
-def deposit_kernel(rows, cols, own_s, own_o, rim_s, rim_o, out_r, out_i):
-    n = own_s.shape[-1]
+def deposit_kernel(section, rows, cols, *refs):
+    pieces, (out_r, out_i) = refs[:8], refs[8:]
+    n = pieces[0].shape[-1]
     span = n + 128
     row_index = lax.broadcasted_iota(jnp.int32, (n, n), 0)
+    first = section[0] == 0
     for ri, out in enumerate((out_r, out_i)):
         out[...] = jnp.zeros_like(out)
-        for k, src in enumerate((own_s, own_o, rim_s, rim_o)):
+        for k in range(4):
             keep = row_index >= rows[k] if k < 2 else row_index < rows[k]
-            term = jnp.where(keep, src[ri, 0], 0.0)
+            term = jnp.where(first, pieces[2 * k][ri, 0], pieces[2 * k + 1][ri, 0])
+            term = jnp.where(keep, term, 0.0)
             base, shift = column_place(cols[k], out.shape[-1], span)
             wide = jnp.concatenate([term, jnp.zeros((n, 128), F32)], 1)
             out[0, :, pl.ds(base, span)] += pltpu.roll(wide, shift, 1)
@@ -156,38 +170,46 @@
     npos, nslab = lax.axis_size("pos"), lax.axis_size("slab")
     section = lax.axis_index("slab")
 
-    def ring_pairs(step, flip):
-        pairs = []
-        for p in range(npos):
-            for s in range(nslab):
-                to = ((p + step) % npos) * nslab + (1 - s if flip else s)
-                pairs.append((p * nslab + s, to))
-        return pairs
-
-    def send(x, step, flip):
-        return lax.ppermute(x, ("pos", "slab"), ring_pairs(step, flip))
-
+    def send(x, step, routes):
+        pairs = [
+            (p * nslab + src, ((p + step) % npos) * nslab + dst)
+            for p in range(npos)
+            for src, dst in routes
+        ]
+        return lax.ppermute(x, ("pos", "slab"), pairs)
+
+    given = jnp.stack([row_off, col_off])
+    tile_before = send(given, 1, ((0, 0), (1, 1)))
     order = jnp.stack([section, 1 - section])
-    mine = jnp.stack([row_off, col_off])[:, order]
-    before = send(mine, 1, False)
+    mine, before = given[:, order], tile_before[:, order]
     rows = jnp.concatenate([mine[0], before[0]])
     cols = jnp.concatenate([mine[1], before[1]])
 
     window = jax.ShapeDtypeStruct((2, depth, n, n), F32)
     window_spec = pl.BlockSpec((2, 1, n, n), lambda d: (0, d, 0, 0))
     plane_spec = pl.BlockSpec((1, tile, cols_all), lambda d: (d, 0, 0))
-    own_s, own_o, halo_s, halo_o = pl.pallas_call(
-        cut_kernel,
-        grid=(depth,),
-        out_shape=[window] * 4,
-        in_specs=[SMEM, plane_spec, plane_spec],
-        out_specs=[window_spec] * 4,
-        compiler_params=pltpu.CompilerParams(vmem_limit_bytes=40 * 2**20),
-        name="cut",
-    )(cols, obj_real, obj_imag)
-    halo_s = send(halo_s, -1, False)
-    halo_o = send(halo_o, -1, True)
-    own_o = send(own_o, 0, True)
+    anywhere = pl.BlockSpec(memory_space=pl.ANY)
+
+    def cut(places, *after):
+        count = places.shape[0]
+        return pl.pallas_call(
+            cut_kernel,
+            grid=(depth,),
+            out_shape=[window] * count,
+            in_specs=[SMEM, plane_spec, plane_spec] + [anywhere] * len(after),
+            out_specs=[window_spec] * count,
+            compiler_params=pltpu.CompilerParams(vmem_limit_bytes=40 * 2**20),
+            cost_estimate=pl.CostEstimate(flops=0, bytes_accessed=8 * 2**20, transcendentals=0),
+            name="cut",
+        )(places, obj_real, obj_imag, *after)
+
+    (first_halo,) = cut(tile_before[1, :1])
+    halos = [[send(first_halo, -1, ((0, 0),)), send(first_halo, -1, ((1, 0),))]]
+    second_halo, own_s, own_o = cut(
+        jnp.concatenate([tile_before[1, 1:], mine[1]]), first_halo
+    )
+    halos.append([send(second_halo, -1, ((1, 1),)), send(second_halo, -1, ((0, 1),))])
+    own_o = send(own_o, 0, ((0, 1), (1, 0)))
 
     half = (taps.shape[1] - 1) // 2
     gap = jnp.zeros((2, 2 * n - taps.shape[1]), F32)
@@ -201,32 +223,45 @@
     )
     info = jnp.stack([section, rows[0]]).astype(jnp.int32)
     square = pltpu.VMEM((2 * n, 2 * n), BF16)
-    term_s, term_o = pl.pallas_call(
-        wave_kernel,
-        out_shape=[window] * 2,
-        in_specs=[SMEM] + [VMEM] * 11,
-        out_specs=[VMEM] * 2,
-        scratch_shapes=[
-            pltpu.VMEM((2 * depth, 2, n, n), F32),
-            pltpu.VMEM((2 * depth + 1, 2, n, n), F32),
-            square, square, square, square,
-        ],
-        compiler_params=pltpu.CompilerParams(vmem_limit_bytes=48 * 2**20),
-        name="waves",
-    )(info, own_s, own_o, halo_s, halo_o, probe, ring, intensity, *fourier_blocks(n))
-
-    rim_s = send(term_s, 1, False)
-    rim_o = send(term_o, 1, True)
-    own_o = send(term_o, 0, True)
+    constants = fourier_blocks(n)
+
+    def waves(phase, *after):
+        return pl.pallas_call(
+            functools.partial(wave_kernel, phase),
+            out_shape=[window] * 2,
+            in_specs=[SMEM] + [VMEM] * 11 + [anywhere] * len(after),
+            out_specs=[VMEM] * 2,
+            scratch_shapes=[
+                pltpu.VMEM((2 * depth, 2, n, n), F32),
+                pltpu.VMEM((2 * depth + 1, 2, n, n), F32),
+                square, square, square, square,
+            ],
+            compiler_params=pltpu.CompilerParams(vmem_limit_bytes=48 * 2**20),
+            cost_estimate=pl.CostEstimate(
+                flops=(8 * depth + 4) * 24 * n**3, bytes_accessed=2**23, transcendentals=0
+            ),
+            name="waves",
+        )(info, own_s, own_o, *halos[phase], probe, ring, intensity, *constants, *after)
+
+    terms = [waves(0)]
+    terms.append(waves(1, terms[0][0]))
+    pieces = [[], [], [], []]
+    for k, (same, other) in enumerate(terms):
+        pieces[0].append(same)
+        pieces[1].append(send(other, 0, ((k, 1 - k),)))
+        pieces[2].append(send(same, 1, ((k, k),)))
+        pieces[3].append(send(other, 1, ((k, 1 - k),)))
+    for k in (1, 3):
+        pieces[k].reverse()
     return pl.pallas_call(
         deposit_kernel,
         grid=(depth,),
         out_shape=[jax.ShapeDtypeStruct(obj_real.shape, F32)] * 2,
-        in_specs=[SMEM, SMEM] + [window_spec] * 4,
+        in_specs=[SMEM] * 3 + [window_spec] * 8,
         out_specs=[plane_spec] * 2,
         compiler_params=pltpu.CompilerParams(vmem_limit_bytes=40 * 2**20),
         name="deposit",
-    )(rows, cols, term_s, own_o, rim_s, rim_o)
+    )(info[:1], rows, cols, *pieces[0], *pieces[1], *pieces[2], *pieces[3])
 
 
 def solution(mesh):

time: 144 us -> 132 us (0.917)
  the two profiles are of different devices: /device:TPU:1 before, /device:TPU:0 now
where the time goes in v2:
time: 132 us; the launch traced here: 131 us
  waiting for transfers between devices  53.8 us (41%)
  Pallas kernels  37 us (28%)
  starting transfers between devices  22.1 us (17%)
  local copies, waits for them, and re-layouts  15.9 us (12%)
  other arithmetic  1.75 us (1%)
    ppermute x12, waiting for transfers between devices, send(): return lax.ppermute(x, ('pos', 'slab'), pairs)  53.8 us
    pallas_call x2, Pallas kernels, waves(): pl.pallas_call(functools.partial(wave_kernel, phase), out_shape=[window]...  27 us
    ppermute x12, starting transfers between devices, send(): return lax.ppermute(x, ('pos', 'slab'), pairs)  22.1 us
    unnamed x40, local copies, waits for them, and re-layouts  11.5 us
    pallas_call x1, Pallas kernels, local(): pl.pallas_call(deposit_kernel, grid=(depth,), out_shape=[jax.ShapeDtypeSt...  5.6 us
    pallas_call x2, Pallas kernels, cut(): pl.pallas_call(cut_kernel, grid=(depth,), out_shape=[window] * count, in_...  4.4 us
  transfers between devices with their start and end apart: 12, of which 6 were waited for; matrix products, arithmetic and copies ran while one was open for 3% of the time, Pallas kernels for 23%

profile of v2, /device:TPU:0, one launch (start us, length us, event | category | flops | bytes accessed | tf_op | source)
XLA Modules:
  0.0 131.5 jit_solution(4448727014400577859)
XLA Ops:
  0.6 0.7 copy.15
  2.2 3.0 %collective-permute-start = (s32[2,2]{0,1:T(2,128)S(1)}, s32[2,2]{0,1:T(2,128)S(1)}, u32[]{:S(2)}, u32[]{:S(2)}) collective-permute-start(s32[2,2]{0,1:T(2,128)S(1)} %pad_add_fusion), channel_id=1, source_target_pairs={{0,2},{1,3},{2,4},{3,5},{4,6},{5,7},{6,8},{7,9},{8,10},{9,11},{10,... | collective-permute-start | bytes 56 | tf_op jit(solution)/shard_map/ppermute | solution.py:179
  6.0 3.8 %collective-permute-done = s32[2,2]{0,1:T(2,128)S(1)} collective-permute-done((s32[2,2]{0,1:T(2,128)S(1)}, s32[2,2]{0,1:T(2,128)S(1)}, u32[]{:S(2)}, u32[]{:S(2)}) %collective-permute-start) | collective-permute-done | bytes 48 | tf_op jit(solution)/shard_map/ppermute | solution.py:179
  10.3 1.6 %copy-done = f32[2,256,1024]{2,1,0:T(8,128)S(1)} copy-done((f32[2,256,1024]{2,1,0:T(8,128)S(1)}, f32[2,256,1024]{2,1,0:T(8,128)}, u32[]{:S(2)}) %copy-start) | copy-done | bytes 2097176
  11.9 1.6 %copy-done.2 = f32[2,256,1024]{2,1,0:T(8,128)S(1)} copy-done((f32[2,256,1024]{2,1,0:T(8,128)S(1)}, f32[2,256,1024]{2,1,0:T(8,128)}, u32[]{:S(2)}) %copy-start.2) | copy-done | bytes 2097176
  13.5 1.5 %cut.2.rest_0_ = f32[2,2,256,256]{3,2,1,0:T(8,128)S(1)} custom-call(s32[1]{0:T(128)} %bitcast.10.cols, f32[2,256,1024]{2,1,0:T(8,128)S(1)} %copy-done, f32[2,256,1024]{2,1,0:T(8,128)S(1)} %copy-done.2), custom_call_target="tpu_custom_call" | custom-call | bytes 8388608 | tf_op jit(solution)/shard_map/cut/pallas_call | solution.py:195
  15.0 1.3 collective-permute-start.3
  16.3 3.9 %collective-permute-start.2 = (f32[2,2,256,256]{3,2,1,0:T(8,128)S(1)}, f32[2,2,256,256]{3,2,1,0:T(8,128)}, u32[]{:S(2)}, u32[]{:S(2)}) collective-permute-start(f32[2,2,256,256]{3,2,1,0:T(8,128)S(1)} %cut.2.rest_0_), channel_id=1, source_target_pairs={{0,14},{2,0},{4,2},{6,4},{8,6},{10,8},{12,10},{14,12},{16,30},{18,... | collective-permute-start | bytes 3145736 | tf_op jit(solution)/shard_map/ppermute | solution.py:179
  21.0 2.9 %cut.3 = (f32[2,2,256,256]{3,2,1,0:T(8,128)}, f32[2,2,256,256]{3,2,1,0:T(8,128)S(1)}, f32[2,2,256,256]{3,2,1,0:T(8,128)S(1)}) custom-call(s32[3]{0:T(128)S(1)} %pad_add_fusion.4.cols, f32[2,256,1024]{2,1,0:T(8,128)S(1)} %copy-done.1, f32[2,256,1024]{2,1,0:T(8,128)S(1)} %copy-done.3, f32[2,2,256,256]{3,2,1,0:T(8,128)S(1)} %cut.2.rest_0_), custom_call_target="tpu_custom_call" | custom-call | bytes 8388608 | tf_op jit(solution)/shard_map/cut/pallas_call | solution.py:195
  23.9 1.0 copy-done.6
  24.9 1.4 %collective-permute-start.1 = (f32[2,2,256,256]{3,2,1,0:T(8,128)S(1)}, f32[2,2,256,256]{3,2,1,0:T(8,128)}, u32[]{:S(2)}, u32[]{:S(2)}) collective-permute-start(f32[2,2,256,256]{3,2,1,0:T(8,128)S(1)} %get-tuple-element.10), channel_id=1, source_target_pairs={{0,1},{1,0},{2,3},{3,2},{4,5},{5,4},{6,7},{7,6},{8,9},{9,8},{10,11... | collective-permute-start | bytes 3145736 | tf_op jit(solution)/shard_map/ppermute | solution.py:179
  28.0 3.0 %collective-permute-start.5 = (f32[2,2,256,256]{3,2,1,0:T(8,128)}, f32[2,2,256,256]{3,2,1,0:T(8,128)S(1)}, u32[]{:S(2)}, u32[]{:S(2)}) collective-permute-start(f32[2,2,256,256]{3,2,1,0:T(8,128)} %get-tuple-element.12), channel_id=1, source_target_pairs={{0,15},{2,1},{4,3},{6,5},{8,7},{10,9},{12,11},{14,13},{16,31},{18,... | collective-permute-start | bytes 3145736 | tf_op jit(solution)/shard_map/ppermute | solution.py:179
  31.7 8.9 %collective-permute-done.3.refs_3_ = f32[2,2,256,256]{3,2,1,0:T(8,128)} collective-permute-done((f32[2,2,256,256]{3,2,1,0:T(8,128)S(1)}, f32[2,2,256,256]{3,2,1,0:T(8,128)}, u32[]{:S(2)}, u32[]{:S(2)}) %collective-permute-start.3) | collective-permute-done | bytes 1048608 | tf_op jit(solution)/shard_map/ppermute | solution.py:179
  40.5 3.9 %collective-permute-done.2.refs_2_ = f32[2,2,256,256]{3,2,1,0:T(8,128)} collective-permute-done((f32[2,2,256,256]{3,2,1,0:T(8,128)S(1)}, f32[2,2,256,256]{3,2,1,0:T(8,128)}, u32[]{:S(2)}, u32[]{:S(2)}) %collective-permute-start.2) | collective-permute-done | bytes 1048608 | tf_op jit(solution)/shard_map/ppermute | solution.py:179
  44.4 1.0 copy-done.11
  45.5 1.0 copy-done.13
  46.5 1.0 copy-done.14
  47.6 1.0 copy-done.15
  48.6 23.2 %waves.2 = (f32[2,2,256,256]{3,2,1,0:T(8,128)S(1)}, f32[2,2,256,256]{3,2,1,0:T(8,128)}) custom-call(s32[2]{0:T(128)S(1)} %pad_add_fusion.3.info, f32[2,2,256,256]{3,2,1,0:T(8,128)} %copy-done.6, f32[2,2,256,256]{3,2,1,0:T(8,128)} %collective-permute-done.1.refs_1_, f32[2,2,256,256]{3,2,1,0:T(8,128)} %collective-permute-done.2.refs_2_, ...), custom_call_target="tpu_custom_call" | custom-call | flops 8053063680 | bytes 8388608 | tf_op jit(solution)/shard_map/waves/pallas_call | solution.py:229
  71.9 1.3 %collective-permute-start.11 = (f32[2,2,256,256]{3,2,1,0:T(8,128)}, f32[2,2,256,256]{3,2,1,0:T(8,128)S(1)}, u32[]{:S(2)}, u32[]{:S(2)}) collective-permute-start(f32[2,2,256,256]{3,2,1,0:T(8,128)} %get-tuple-element.15), channel_id=1, source_target_pairs={{0,3},{2,5},{4,7},{6,9},{8,11},{10,13},{12,15},{14,1},{16,19},{18,... | collective-permute-start | bytes 3145736 | tf_op jit(solution)/shard_map/ppermute | solution.py:179
  73.2 1.4 %collective-permute-start.7 = (f32[2,2,256,256]{3,2,1,0:T(8,128)}, f32[2,2,256,256]{3,2,1,0:T(8,128)S(1)}, u32[]{:S(2)}, u32[]{:S(2)}) collective-permute-start(f32[2,2,256,256]{3,2,1,0:T(8,128)} %get-tuple-element.15), channel_id=1, source_target_pairs={{0,1},{2,3},{4,5},{6,7},{8,9},{10,11},{12,13},{14,15},{16,17},{18,... | collective-permute-start | bytes 3145736 | tf_op jit(solution)/shard_map/ppermute | solution.py:179
  74.6 1.9 %collective-permute-start.8 = (f32[2,2,256,256]{3,2,1,0:T(8,128)S(1)}, f32[2,2,256,256]{3,2,1,0:T(8,128)}, u32[]{:S(2)}, u32[]{:S(2)}) collective-permute-start(f32[2,2,256,256]{3,2,1,0:T(8,128)S(1)} %get-tuple-element.11.refs_11_.refs_0_), channel_id=1, source_target_pairs={{0,2},{2,4},{4,6},{6,8},{8,10},{10,12},{12,14},{14,0},{16,18},{18,... | collective-permute-start | bytes 3145736 | tf_op jit(solution)/shard_map/ppermute | solution.py:179
  76.5 1.0 copy-done.18
  77.5 1.0 copy-done.19
  78.5 3.8 %waves.3 = (f32[2,2,256,256]{3,2,1,0:T(8,128)}, f32[2,2,256,256]{3,2,1,0:T(8,128)}) custom-call(s32[2]{0:T(128)S(1)} %pad_add_fusion.3.info, f32[2,2,256,256]{3,2,1,0:T(8,128)} %copy-done.6, f32[2,2,256,256]{3,2,1,0:T(8,128)} %collective-permute-done.1.refs_1_, f32[2,2,256,256]{3,2,1,0:T(8,128)} %copy-done.19, f32[2,2,256,256]{3,2,1,0:T(8,128)} %copy-done.18, ...), custom_call_target="tpu_custom_call" | custom-call | flops 8053063680 | bytes 8388608 | tf_op jit(solution)/shard_map/waves/pallas_call | solution.py:229
  82.3 1.6 %collective-permute-start.9 = (f32[2,2,256,256]{3,2,1,0:T(8,128)}, f32[2,2,256,256]{3,2,1,0:T(8,128)}, u32[]{:S(2)}, u32[]{:S(2)}) collective-permute-start(f32[2,2,256,256]{3,2,1,0:T(8,128)} %get-tuple-element.13.refs_1_), channel_id=1, source_target_pairs={{1,3},{3,5},{5,7},{7,9},{9,11},{11,13},{13,15},{15,1},{17,19},{19,... | collective-permute-start | bytes 3145736 | tf_op jit(solution)/shard_map/ppermute | solution.py:179
  83.9 1.3 collective-permute-start.10
  85.8 1.3 collective-permute-start.6
  87.9 18.3 %collective-permute-done.8.refs_4_ = f32[2,2,256,256]{3,2,1,0:T(8,128)} collective-permute-done((f32[2,2,256,256]{3,2,1,0:T(8,128)S(1)}, f32[2,2,256,256]{3,2,1,0:T(8,128)}, u32[]{:S(2)}, u32[]{:S(2)}) %collective-permute-start.8) | collective-permute-done | bytes 1048608 | tf_op jit(solution)/shard_map/ppermute | solution.py:179
  106.1 18.5 %collective-permute-done.10.refs_6_ = f32[2,2,256,256]{3,2,1,0:T(8,128)} collective-permute-done((f32[2,2,256,256]{3,2,1,0:T(8,128)}, f32[2,2,256,256]{3,2,1,0:T(8,128)}, u32[]{:S(2)}, u32[]{:S(2)}) %collective-permute-start.10) | collective-permute-done | bytes 1048608 | tf_op jit(solution)/shard_map/ppermute | solution.py:179
  124.6 1.2 copy-done.5
  125.9 5.6 %deposit.1 = (f32[2,256,1024]{2,1,0:T(8,128)}, f32[2,256,1024]{2,1,0:T(8,128)}) custom-call(s32[1]{0:T(128)} %bitcast.section, s32[4]{0:T(128)S(1)} %get-tuple-element.26.rows, s32[4]{0:T(128)S(1)} %get-tuple-element.27.cols, f32[2,2,256,256]{3,2,1,0:T(8,128)S(1)} %copy-done.5, f32[2,2,256,256]{3,2,1,0:T(8,128)} %get-tuple-element.13.refs_1_, ...), custom_call_target="tpu_custom_call" | custom-call | tf_op jit(solution)/shard_map/deposit/pallas_call | solution.py:256
  (57 shorter events, 6.8 us)
Async XLA Ops:
  2.2 7.6 %collective-permute-start = (s32[2,2]{0,1:T(2,128)S(1)}, s32[2,2]{0,1:T(2,128)S(1)}, u32[]{:S(2)}, u32[]{:S(2)}) collective-permute-start(s32[2,2]{0,1:T(2,128)S(1)} %pad_add_fusion), channel_id=1, source_target_pairs={{0,2},{1,3},{2,4},{3,5},{4,6},{5,7},{6,8},{7,9},{8,10},{9,11},{10,... | collective-permute-start | bytes 56 | tf_op jit(solution)/shard_map/ppermute | solution.py:179
  10.3 1.6 %copy-start = (f32[2,256,1024]{2,1,0:T(8,128)S(1)}, f32[2,256,1024]{2,1,0:T(8,128)}, u32[]{:S(2)}) copy-start(f32[2,256,1024]{2,1,0:T(8,128)} %obj_r.3) | copy-start | bytes 6291460
  11.9 1.6 %copy-start.2 = (f32[2,256,1024]{2,1,0:T(8,128)S(1)}, f32[2,256,1024]{2,1,0:T(8,128)}, u32[]{:S(2)}) copy-start(f32[2,256,1024]{2,1,0:T(8,128)} %obj_i.3) | copy-start | bytes 6291460
  13.5 7.5 %copy-start.1 = (f32[2,256,1024]{2,1,0:T(8,128)S(1)}, f32[2,256,1024]{2,1,0:T(8,128)}, u32[]{:S(2)}) copy-start(f32[2,256,1024]{2,1,0:T(8,128)} %obj_r.3) | copy-start | bytes 6291460
  13.5 7.5 %copy-start.3 = (f32[2,256,1024]{2,1,0:T(8,128)S(1)}, f32[2,256,1024]{2,1,0:T(8,128)}, u32[]{:S(2)}) copy-start(f32[2,256,1024]{2,1,0:T(8,128)} %obj_i.3) | copy-start | bytes 6291460
  15.0 25.5 %collective-permute-start.3 = (f32[2,2,256,256]{3,2,1,0:T(8,128)S(1)}, f32[2,2,256,256]{3,2,1,0:T(8,128)}, u32[]{:S(2)}, u32[]{:S(2)}) collective-permute-start(f32[2,2,256,256]{3,2,1,0:T(8,128)S(1)} %cut.2.rest_0_), channel_id=1, source_target_pairs={{1,14},{3,0},{5,2},{7,4},{9,6},{11,8},{13,10},{15,12},{17,30},{19,... | collective-permute-start | bytes 3145736 | tf_op jit(solution)/shard_map/ppermute | solution.py:179
  16.3 28.1 %collective-permute-start.2 = (f32[2,2,256,256]{3,2,1,0:T(8,128)S(1)}, f32[2,2,256,256]{3,2,1,0:T(8,128)}, u32[]{:S(2)}, u32[]{:S(2)}) collective-permute-start(f32[2,2,256,256]{3,2,1,0:T(8,128)S(1)} %cut.2.rest_0_), channel_id=1, source_target_pairs={{0,14},{2,0},{4,2},{6,4},{8,6},{10,8},{12,10},{14,12},{16,30},{18,... | collective-permute-start | bytes 3145736 | tf_op jit(solution)/shard_map/ppermute | solution.py:179
  21.0 5.8 %copy-start.17 = (f32[2,63]{1,0:T(2,128)S(1)}, f32[2,63]{1,0:T(2,128)}, u32[]{:S(2)}) copy-start(f32[2,63]{1,0:T(2,128)} %param.14) | copy-start | bytes 1516
  21.0 23.4 %copy-start.7 = (f32[2,256,256]{2,1,0:T(8,128)S(1)}, f32[2,256,256]{2,1,0:T(8,128)}, u32[]{:S(2)}) copy-start(f32[2,256,256]{2,1,0:T(8,128)} %refs_4_.3) | copy-start | bytes 1572868
  21.0 23.4 %copy-start.9 = (f32[2,256,256]{2,1,0:T(8,128)S(1)}, f32[2,256,256]{2,1,0:T(8,128)}, u32[]{:S(2)}) copy-start(f32[2,256,256]{2,1,0:T(8,128)} %refs_6_.3) | copy-start | bytes 1572868
  23.9 1.0 copy-start.6
  24.9 19.5 %collective-permute-start.1 = (f32[2,2,256,256]{3,2,1,0:T(8,128)S(1)}, f32[2,2,256,256]{3,2,1,0:T(8,128)}, u32[]{:S(2)}, u32[]{:S(2)}) collective-permute-start(f32[2,2,256,256]{3,2,1,0:T(8,128)S(1)} %get-tuple-element.10), channel_id=1, source_target_pairs={{0,1},{1,0},{2,3},{3,2},{4,5},{5,4},{6,7},{7,6},{8,9},{9,8},{10,11... | collective-permute-start | bytes 3145736 | tf_op jit(solution)/shard_map/ppermute | solution.py:179
  28.0 48.6 %collective-permute-start.5 = (f32[2,2,256,256]{3,2,1,0:T(8,128)}, f32[2,2,256,256]{3,2,1,0:T(8,128)S(1)}, u32[]{:S(2)}, u32[]{:S(2)}) collective-permute-start(f32[2,2,256,256]{3,2,1,0:T(8,128)} %get-tuple-element.12), channel_id=1, source_target_pairs={{0,15},{2,1},{4,3},{6,5},{8,7},{10,9},{12,11},{14,13},{16,31},{18,... | collective-permute-start | bytes 3145736 | tf_op jit(solution)/shard_map/ppermute | solution.py:179
  30.9 45.6 %collective-permute-start.4 = (f32[2,2,256,256]{3,2,1,0:T(8,128)}, f32[2,2,256,256]{3,2,1,0:T(8,128)S(1)}, u32[]{:S(2)}, u32[]{:S(2)}) collective-permute-start(f32[2,2,256,256]{3,2,1,0:T(8,128)} %get-tuple-element.12), channel_id=1, source_target_pairs={{1,15},{3,1},{5,3},{7,5},{9,7},{11,9},{13,11},{15,13},{17,31},{19,... | collective-permute-start | bytes 3145736 | tf_op jit(solution)/shard_map/ppermute | solution.py:179
  44.4 1.0 copy-start.11
  45.5 1.0 copy-start.13
  46.5 1.0 copy-start.14
  47.6 1.0 copy-start.15
  48.6 29.9 %copy-start.8 = (f32[2,256,256]{2,1,0:T(8,128)S(1)}, f32[2,256,256]{2,1,0:T(8,128)}, u32[]{:S(2)}) copy-start(f32[2,256,256]{2,1,0:T(8,128)} %refs_4_.3) | copy-start | bytes 1572868
  48.6 29.9 %copy-start.10 = (f32[2,256,256]{2,1,0:T(8,128)S(1)}, f32[2,256,256]{2,1,0:T(8,128)}, u32[]{:S(2)}) copy-start(f32[2,256,256]{2,1,0:T(8,128)} %refs_6_.3) | copy-start | bytes 1572868
  48.6 29.9 %copy-start.12 = (bf16[512,512]{1,0:T(8,128)(2,1)S(1)}, bf16[512,512]{1,0:T(8,128)(2,1)}, u32[]{:S(2)}) copy-start(bf16[512,512]{1,0:T(8,128)(2,1)} %constant.23.clone.refs_10_) | copy-start | bytes 1572868
  48.6 29.9 %copy-start.16 = (bf16[512,512]{1,0:T(8,128)(2,1)S(1)}, bf16[512,512]{1,0:T(8,128)(2,1)}, u32[]{:S(2)}) copy-start(bf16[512,512]{1,0:T(8,128)(2,1)} %constant.20.clone.refs_7_) | copy-start | bytes 1572868
  71.9 4.7 %copy-start.4 = (f32[2,2,256,256]{3,2,1,0:T(8,128)}, f32[2,2,256,256]{3,2,1,0:T(8,128)S(1)}, u32[]{:S(2)}) copy-start(f32[2,2,256,256]{3,2,1,0:T(8,128)S(1)} %get-tuple-element.11.refs_11_.refs_0_) | copy-start | bytes 3145732
  71.9 13.9 %collective-permute-start.11 = (f32[2,2,256,256]{3,2,1,0:T(8,128)}, f32[2,2,256,256]{3,2,1,0:T(8,128)S(1)}, u32[]{:S(2)}, u32[]{:S(2)}) collective-permute-start(f32[2,2,256,256]{3,2,1,0:T(8,128)} %get-tuple-element.15), channel_id=1, source_target_pairs={{0,3},{2,5},{4,7},{6,9},{8,11},{10,13},{12,15},{14,1},{16,19},{18,... | collective-permute-start | bytes 3145736 | tf_op jit(solution)/shard_map/ppermute | solution.py:179
  73.2 14.7 %collective-permute-start.7 = (f32[2,2,256,256]{3,2,1,0:T(8,128)}, f32[2,2,256,256]{3,2,1,0:T(8,128)S(1)}, u32[]{:S(2)}, u32[]{:S(2)}) collective-permute-start(f32[2,2,256,256]{3,2,1,0:T(8,128)} %get-tuple-element.15), channel_id=1, source_target_pairs={{0,1},{2,3},{4,5},{6,7},{8,9},{10,11},{12,13},{14,15},{16,17},{18,... | collective-permute-start | bytes 3145736 | tf_op jit(solution)/shard_map/ppermute | solution.py:179
  74.6 31.6 %collective-permute-start.8 = (f32[2,2,256,256]{3,2,1,0:T(8,128)S(1)}, f32[2,2,256,256]{3,2,1,0:T(8,128)}, u32[]{:S(2)}, u32[]{:S(2)}) collective-permute-start(f32[2,2,256,256]{3,2,1,0:T(8,128)S(1)} %get-tuple-element.11.refs_11_.refs_0_), channel_id=1, source_target_pairs={{0,2},{2,4},{4,6},{6,8},{8,10},{10,12},{12,14},{14,0},{16,18},{18,... | collective-permute-start | bytes 3145736 | tf_op jit(solution)/shard_map/ppermute | solution.py:179
  76.5 1.0 copy-start.18
  77.5 1.0 copy-start.19
  82.3 23.9 %collective-permute-start.9 = (f32[2,2,256,256]{3,2,1,0:T(8,128)}, f32[2,2,256,256]{3,2,1,0:T(8,128)}, u32[]{:S(2)}, u32[]{:S(2)}) collective-permute-start(f32[2,2,256,256]{3,2,1,0:T(8,128)} %get-tuple-element.13.refs_1_), channel_id=1, source_target_pairs={{1,3},{3,5},{5,7},{7,9},{9,11},{11,13},{13,15},{15,1},{17,19},{19,... | collective-permute-start | bytes 3145736 | tf_op jit(solution)/shard_map/ppermute | solution.py:179
  83.9 40.7 %collective-permute-start.10 = (f32[2,2,256,256]{3,2,1,0:T(8,128)}, f32[2,2,256,256]{3,2,1,0:T(8,128)}, u32[]{:S(2)}, u32[]{:S(2)}) collective-permute-start(f32[2,2,256,256]{3,2,1,0:T(8,128)} %get-tuple-element.14), channel_id=1, source_target_pairs={{1,2},{3,4},{5,6},{7,8},{9,10},{11,12},{13,14},{15,0},{17,18},{19,... | collective-permute-start | bytes 3145736 | tf_op jit(solution)/shard_map/ppermute | solution.py:179
  85.8 38.9 %collective-permute-start.6 = (f32[2,2,256,256]{3,2,1,0:T(8,128)}, f32[2,2,256,256]{3,2,1,0:T(8,128)}, u32[]{:S(2)}, u32[]{:S(2)}) collective-permute-start(f32[2,2,256,256]{3,2,1,0:T(8,128)} %get-tuple-element.14), channel_id=1, source_target_pairs={{1,0},{3,2},{5,4},{7,6},{9,8},{11,10},{13,12},{15,14},{17,16},{19,... | collective-permute-start | bytes 3145736 | tf_op jit(solution)/shard_map/ppermute | solution.py:179
  124.6 1.2 copy-start.5

commit v3 on v2

--- a/solution.py
+++ b/solution.py
@@ -52,7 +52,7 @@
     for m in (c, d):
         high = m.astype(jnp.bfloat16)
         out += [high, (m - high.astype(np.float32)).astype(jnp.bfloat16)]
-    return [jnp.asarray(m) for m in out]
+    return jnp.asarray(np.stack(out))
 
 
 def column_place(col, cols_all, span):
@@ -71,9 +71,23 @@
             out[ri, 0] = pltpu.roll(wide, lax.rem(span - shift, span), 1)[:, :n]
 
 
+def band_kernel(ring, out):
+    n = out.shape[-1] // 2
+
+    def toeplitz(k):
+        rows = jnp.broadcast_to(ring[k : k + 1, :], (n, 2 * n))
+        return pltpu.roll(rows, 0, 1, stride=1, stride_axis=0)[:, :n]
+
+    for k, kr, ki in ((0, toeplitz(0), -toeplitz(1)), (2, toeplitz(2), toeplitz(3))):
+        for r0, c0, block in ((0, 0, kr), (0, n, ki), (n, 0, -ki), (n, n, kr)):
+            hi, lo = halves(block)
+            out[k, r0 : r0 + n, c0 : c0 + n] = hi
+            out[k + 1, r0 : r0 + n, c0 : c0 + n] = lo
+
+
 def wave_kernel(phase, info, *refs):
     if phase > 0:
-        refs = refs[:11] + refs[12:]
+        refs = refs[:8] + refs[9:]
 
     @pl.when(info[0] == phase)
     def _():
@@ -81,70 +95,88 @@
 
 
 def wave_body(
-    info, own_s, own_o, halo_s, halo_o, probe, ring, intensity, ch, cl, dh, dl,
-    term_s, term_o, patch, waves, ah, al, bh, bl,
+    info, own_s, own_o, halo_s, halo_o, probe, intensity, bands, fourier, term_s, term_o,
+    own, halo, patch, waves, measured, band, dft, in_sem, out_sem, side_sem,
 ):
     n = probe.shape[-1]
     depth = own_s.shape[1]
+    slices = 2 * depth
     section, row = info[0], info[1]
     unroll_by = lax.rem(n - row, n)
     from_next = lax.broadcasted_iota(jnp.int32, (n, n), 0) < row
-    for own, halo, where in ((own_s, halo_s, section), (own_o, halo_o, 1 - section)):
-        for d in range(depth):
-            for ri in range(2):
-                merged = jnp.where(from_next, halo[ri, d], own[ri, d])
-                patch[where * depth + d, ri] = pltpu.roll(merged, unroll_by, 0)
-
-    def toeplitz(k):
-        rows = jnp.broadcast_to(ring[k : k + 1, :], (n, 2 * n))
-        return pltpu.roll(rows, 0, 1, stride=1, stride_axis=0)[:, :n]
-
-    for high, low, kr, ki in ((ah, al, toeplitz(0), -toeplitz(1)), (bh, bl, toeplitz(2), toeplitz(3))):
-        for r0, c0, block in ((0, 0, kr), (0, n, ki), (n, 0, -ki), (n, n, kr)):
-            hi, lo = halves(block)
-            high[r0 : r0 + n, c0 : c0 + n] = hi
-            low[r0 : r0 + n, c0 : c0 + n] = lo
-
-    waves[0] = probe[...]
-    slices = 2 * depth
+
+    lead = pltpu.make_async_copy(probe, waves.at[0], side_sem.at[0])
+    band_in = pltpu.make_async_copy(bands, band, side_sem.at[1])
+    dft_in = pltpu.make_async_copy(fourier, dft, side_sem.at[2])
+    measured_in = pltpu.make_async_copy(intensity.at[section], measured, side_sem.at[3])
+
+    def incoming(source, target, kind, slot, d):
+        return pltpu.make_async_copy(source.at[:, d], target.at[slot], in_sem.at[kind, slot])
+
+    lead.start()
+    band_in.start()
+    for d in range(depth):
+        for o, h, where in ((own_s, halo_s, section), (own_o, halo_o, 1 - section)):
+            incoming(o, own, 0, where * depth + d, d).start()
+            incoming(h, halo, 1, where * depth + d, d).start()
+    dft_in.start()
+    measured_in.start()
+    lead.wait()
+    band_in.wait()
 
     def forward(s, _):
+        incoming(own_s, own, 0, s, 0).wait()
+        incoming(halo_s, halo, 1, s, 0).wait()
+        for ri in range(2):
+            merged = jnp.where(from_next, halo[s, ri], own[s, ri])
+            patch[s, ri] = pltpu.roll(merged, unroll_by, 0)
         pr, pi = waves[s, 0], waves[s, 1]
         o_r, o_i = patch[s, 0], patch[s, 1]
         zr, zi = sandwich(
-            ah[...], al[...], pr * o_r - pi * o_i, pr * o_i + pi * o_r, bh[...], bl[...]
+            band[0], band[1], pr * o_r - pi * o_i, pr * o_i + pi * o_r, band[2], band[3]
         )
         waves[s + 1, 0] = zr
         waves[s + 1, 1] = zi
         return 0
 
     lax.fori_loop(0, slices, forward, 0)
-    fr, fi = sandwich(
-        ch[...], cl[...], waves[slices, 0], waves[slices, 1], dh[...], dl[...]
-    )
-    residual = 2.0 * (fr * fr + fi * fi - intensity[section])
-    xr, xi = sandwich(dh[...], dl[...], residual * fr, residual * fi, ch[...], cl[...])
+    dft_in.wait()
+    measured_in.wait()
+    fr, fi = sandwich(dft[0], dft[1], waves[slices, 0], waves[slices, 1], dft[2], dft[3])
+    residual = 2.0 * (fr * fr + fi * fi - measured[...])
+    xr, xi = sandwich(dft[2], dft[3], residual * fr, residual * fi, dft[0], dft[1])
     waves[slices, 0] = xr
     waves[slices, 1] = xi
+
+    def outgoing(slot, out, d):
+        return pltpu.make_async_copy(own.at[slot], out.at[:, d], out_sem.at[slot])
 
     def backward(t, _):
         s = slices - 1 - t
         a_r, a_i = sandwich(
-            bh[...], bl[...], waves[s + 1, 0], waves[s + 1, 1], ah[...], al[...]
+            band[2], band[3], waves[s + 1, 0], waves[s + 1, 1], band[0], band[1]
         )
         w_r, w_i = waves[s, 0], waves[s, 1]
         o_r, o_i = patch[s, 0], patch[s, 1]
-        patch[s, 0] = a_r * w_r + a_i * w_i
-        patch[s, 1] = a_i * w_r - a_r * w_i
+        own[s, 0] = pltpu.roll(a_r * w_r + a_i * w_i, row, 0)
+        own[s, 1] = pltpu.roll(a_i * w_r - a_r * w_i, row, 0)
         waves[s, 0] = a_r * o_r + a_i * o_i
         waves[s, 1] = a_i * o_r - a_r * o_i
+        group = s // depth
+
+        @pl.when(group == section)
+        def _():
+            outgoing(s, term_s, s - group * depth).start()
+
+        @pl.when(group != section)
+        def _():
+            outgoing(s, term_o, s - group * depth).start()
+
         return 0
 
     lax.fori_loop(0, slices, backward, 0)
-    for out, where in ((term_s, section), (term_o, 1 - section)):
-        for d in range(depth):
-            for ri in range(2):
-                out[ri, d] = pltpu.roll(patch[where * depth + d, ri], row, 0)
+    for s in range(slices):
+        outgoing(s, term_s, 0).wait()
 
 
 def deposit_kernel(section, rows, cols, *refs):
@@ -222,33 +254,47 @@
         0,
     )
     info = jnp.stack([section, rows[0]]).astype(jnp.int32)
-    square = pltpu.VMEM((2 * n, 2 * n), BF16)
-    constants = fourier_blocks(n)
+    fourier = fourier_blocks(n)
+    bands = pl.pallas_call(
+        band_kernel,
+        out_shape=jax.ShapeDtypeStruct((4, 2 * n, 2 * n), BF16),
+        in_specs=[VMEM],
+        out_specs=VMEM,
+        compiler_params=pltpu.CompilerParams(vmem_limit_bytes=40 * 2**20),
+        name="band",
+    )(ring)
 
     def waves(phase, *after):
+        stack = pltpu.VMEM((2 * depth, 2, n, n), F32)
+        matrices = pltpu.VMEM((4, 2 * n, 2 * n), BF16)
         return pl.pallas_call(
             functools.partial(wave_kernel, phase),
             out_shape=[window] * 2,
-            in_specs=[SMEM] + [VMEM] * 11 + [anywhere] * len(after),
-            out_specs=[VMEM] * 2,
+            in_specs=[SMEM] + [anywhere] * (8 + len(after)),
+            out_specs=[anywhere] * 2,
             scratch_shapes=[
-                pltpu.VMEM((2 * depth, 2, n, n), F32),
+                stack, stack, stack,
                 pltpu.VMEM((2 * depth + 1, 2, n, n), F32),
-                square, square, square, square,
+                pltpu.VMEM((n, n), F32),
+                matrices, matrices,
+                pltpu.SemaphoreType.DMA((2, 2 * depth)),
+                pltpu.SemaphoreType.DMA((2 * depth,)),
+                pltpu.SemaphoreType.DMA((4,)),
             ],
-            compiler_params=pltpu.CompilerParams(vmem_limit_bytes=48 * 2**20),
+            compiler_params=pltpu.CompilerParams(vmem_limit_bytes=44 * 2**20),
             cost_estimate=pl.CostEstimate(
                 flops=(8 * depth + 4) * 24 * n**3, bytes_accessed=2**23, transcendentals=0
             ),
             name="waves",
-        )(info, own_s, own_o, *halos[phase], probe, ring, intensity, *constants, *after)
+        )(info, own_s, own_o, *halos[phase], probe, intensity, bands, fourier, *after)
 
     terms = [waves(0)]
-    terms.append(waves(1, terms[0][0]))
+    swapped = send(terms[0][1], 0, ((0, 1),))
+    terms.append(waves(1, swapped))
     pieces = [[], [], [], []]
     for k, (same, other) in enumerate(terms):
         pieces[0].append(same)
-        pieces[1].append(send(other, 0, ((k, 1 - k),)))
+        pieces[1].append(swapped if k == 0 else send(other, 0, ((k, 1 - k),)))
         pieces[2].append(send(same, 1, ((k, k),)))
         pieces[3].append(send(other, 1, ((k, 1 - k),)))
     for k in (1, 3):

time: 132 us -> 138 us (1.045)
  the two profiles are of different devices: /device:TPU:0 before, /device:TPU:1 now
where the time goes in v3:
time: 138 us
  waiting for transfers between devices  62.4 us (45%)
  Pallas kernels  34.2 us (25%)
  starting transfers between devices  26.2 us (19%)
  local copies, waits for them, and re-layouts  11.7 us (8%)
  other arithmetic  2.23 us (2%)
    ppermute x12, waiting for transfers between devices, send(): return lax.ppermute(x, ('pos', 'slab'), pairs)  62.4 us
    ppermute x12, starting transfers between devices, send(): return lax.ppermute(x, ('pos', 'slab'), pairs)  26.2 us
    pallas_call x2, Pallas kernels, waves(): pl.pallas_call(functools.partial(wave_kernel, phase), out_shape=[window]...  23.8 us
    unnamed x28, local copies, waits for them, and re-layouts  7.35 us
    pallas_call x1, Pallas kernels, local(): pl.pallas_call(deposit_kernel, grid=(depth,), out_shape=[jax.ShapeDtypeSt...  5.61 us
    pallas_call x2, Pallas kernels, cut(): pl.pallas_call(cut_kernel, grid=(depth,), out_shape=[window] * count, in_...  4.43 us
  transfers between devices with their start and end apart: 12, of which 6 were waited for; matrix products, arithmetic and copies ran while one was open for 3% of the time, Pallas kernels for 18%

profile of v3, /device:TPU:1, one launch (start us, length us, event | category | flops | bytes accessed | tf_op | source)
XLA Modules:
  0.0 137.5 jit_solution(10238726187123119963)
XLA Ops:
  0.6 0.7 copy.12
  1.4 0.7 copy.13
  2.2 2.1 %collective-permute-start = (s32[2,2]{0,1:T(2,128)S(1)}, s32[2,2]{0,1:T(2,128)S(1)}, u32[]{:S(2)}, u32[]{:S(2)}) collective-permute-start(s32[2,2]{0,1:T(2,128)S(1)} %pad_add_fusion), channel_id=1, source_target_pairs={{0,2},{1,3},{2,4},{3,5},{4,6},{5,7},{6,8},{7,9},{8,10},{9,11},{10,... | collective-permute-start | bytes 56 | tf_op jit(solution)/shard_map/ppermute | solution.py:211
  5.1 3.2 %collective-permute-done = s32[2,2]{0,1:T(2,128)S(1)} collective-permute-done((s32[2,2]{0,1:T(2,128)S(1)}, s32[2,2]{0,1:T(2,128)S(1)}, u32[]{:S(2)}, u32[]{:S(2)}) %collective-permute-start) | collective-permute-done | bytes 48 | tf_op jit(solution)/shard_map/ppermute | solution.py:211
  8.8 0.7 pad_add_fusion.4.cols
  9.6 1.6 %copy-done = f32[2,256,1024]{2,1,0:T(8,128)S(1)} copy-done((f32[2,256,1024]{2,1,0:T(8,128)S(1)}, f32[2,256,1024]{2,1,0:T(8,128)}, u32[]{:S(2)}) %copy-start) | copy-done | bytes 2097176
  11.2 1.6 %copy-done.2 = f32[2,256,1024]{2,1,0:T(8,128)S(1)} copy-done((f32[2,256,1024]{2,1,0:T(8,128)S(1)}, f32[2,256,1024]{2,1,0:T(8,128)}, u32[]{:S(2)}) %copy-start.2) | copy-done | bytes 2097176
  12.7 1.5 %cut.2.rest_0_ = f32[2,2,256,256]{3,2,1,0:T(8,128)S(1)} custom-call(s32[1]{0:T(128)} %bitcast.10.cols, f32[2,256,1024]{2,1,0:T(8,128)S(1)} %copy-done, f32[2,256,1024]{2,1,0:T(8,128)S(1)} %copy-done.2), custom_call_target="tpu_custom_call" | custom-call | bytes 8388608 | tf_op jit(solution)/shard_map/cut/pallas_call | solution.py:227
  15.0 2.9 %cut.3 = (f32[2,2,256,256]{3,2,1,0:T(8,128)S(1)}, f32[2,2,256,256]{3,2,1,0:T(8,128)S(1)}, f32[2,2,256,256]{3,2,1,0:T(8,128)}) custom-call(s32[3]{0:T(128)S(1)} %pad_add_fusion.4.cols, f32[2,256,1024]{2,1,0:T(8,128)S(1)} %copy-done.1, f32[2,256,1024]{2,1,0:T(8,128)S(1)} %copy-done.3, f32[2,2,256,256]{3,2,1,0:T(8,128)S(1)} %cut.2.rest_0_), custom_call_target="tpu_custom_call" | custom-call | bytes 8388608 | tf_op jit(solution)/shard_map/cut/pallas_call | solution.py:227
  17.9 1.0 copy-done.9
  18.9 1.6 %collective-permute-start.1 = (f32[2,2,256,256]{3,2,1,0:T(8,128)}, f32[2,2,256,256]{3,2,1,0:T(8,128)S(1)}, u32[]{:S(2)}, u32[]{:S(2)}) collective-permute-start(f32[2,2,256,256]{3,2,1,0:T(8,128)} %get-tuple-element.10), channel_id=1, source_target_pairs={{0,1},{1,0},{2,3},{3,2},{4,5},{5,4},{6,7},{7,6},{8,9},{9,8},{10,11... | collective-permute-start | bytes 3145736 | tf_op jit(solution)/shard_map/ppermute | solution.py:211
  20.4 1.6 %collective-permute-start.2 = (f32[2,2,256,256]{3,2,1,0:T(8,128)S(1)}, f32[2,2,256,256]{3,2,1,0:T(8,128)}, u32[]{:S(2)}, u32[]{:S(2)}) collective-permute-start(f32[2,2,256,256]{3,2,1,0:T(8,128)S(1)} %cut.2.rest_0_), channel_id=1, source_target_pairs={{0,14},{2,0},{4,2},{6,4},{8,6},{10,8},{12,10},{14,12},{16,30},{18,... | collective-permute-start | bytes 3145736 | tf_op jit(solution)/shard_map/ppermute | solution.py:211
  22.1 6.2 %collective-permute-start.3 = (f32[2,2,256,256]{3,2,1,0:T(8,128)S(1)}, f32[2,2,256,256]{3,2,1,0:T(8,128)}, u32[]{:S(2)}, u32[]{:S(2)}) collective-permute-start(f32[2,2,256,256]{3,2,1,0:T(8,128)S(1)} %cut.2.rest_0_), channel_id=1, source_target_pairs={{1,14},{3,0},{5,2},{7,4},{9,6},{11,8},{13,10},{15,12},{17,30},{19,... | collective-permute-start | bytes 3145736 | tf_op jit(solution)/shard_map/ppermute | solution.py:211
  29.6 1.2 pad_add_fusion.3.info
  30.8 2.1 %collective-permute-start.4 = (f32[2,2,256,256]{3,2,1,0:T(8,128)S(1)}, f32[2,2,256,256]{3,2,1,0:T(8,128)S(1)}, u32[]{:S(2)}, u32[]{:S(2)}) collective-permute-start(f32[2,2,256,256]{3,2,1,0:T(8,128)S(1)} %copy-done.10), channel_id=1, source_target_pairs={{1,15},{3,1},{5,3},{7,5},{9,7},{11,9},{13,11},{15,13},{17,31},{19,... | collective-permute-start | bytes 3145736 | tf_op jit(solution)/shard_map/ppermute | solution.py:211
  32.9 1.3 collective-permute-start.5
  34.2 16.1 %collective-permute-done.3.refs_3_ = f32[2,2,256,256]{3,2,1,0:T(8,128)} collective-permute-done((f32[2,2,256,256]{3,2,1,0:T(8,128)S(1)}, f32[2,2,256,256]{3,2,1,0:T(8,128)}, u32[]{:S(2)}, u32[]{:S(2)}) %collective-permute-start.3) | collective-permute-done | bytes 1048608 | tf_op jit(solution)/shard_map/ppermute | solution.py:211
  50.3 0.7 waves.2
  51.0 1.3 collective-permute-start.6
  52.3 1.3 collective-permute-start.11
  53.6 1.6 %collective-permute-start.8 = (f32[2,2,256,256]{3,2,1,0:T(8,128)S(1)}, f32[2,2,256,256]{3,2,1,0:T(8,128)}, u32[]{:S(2)}, u32[]{:S(2)}) collective-permute-start(f32[2,2,256,256]{3,2,1,0:T(8,128)S(1)} %get-tuple-element.11.refs_0_), channel_id=1, source_target_pairs={{0,2},{2,4},{4,6},{6,8},{8,10},{10,12},{12,14},{14,0},{16,18},{18,... | collective-permute-start | bytes 3145736 | tf_op jit(solution)/shard_map/ppermute | solution.py:211
  55.3 14.9 %collective-permute-done.4.refs_2_ = f32[2,2,256,256]{3,2,1,0:T(8,128)S(1)} collective-permute-done((f32[2,2,256,256]{3,2,1,0:T(8,128)S(1)}, f32[2,2,256,256]{3,2,1,0:T(8,128)S(1)}, u32[]{:S(2)}, u32[]{:S(2)}) %collective-permute-start.4) | collective-permute-done | bytes 1048608 | tf_op jit(solution)/shard_map/ppermute | solution.py:211
  70.1 7.3 %collective-permute-done.6.refs_8_.refs_3_ = f32[2,2,256,256]{3,2,1,0:T(8,128)S(1)} collective-permute-done((f32[2,2,256,256]{3,2,1,0:T(8,128)}, f32[2,2,256,256]{3,2,1,0:T(8,128)S(1)}, u32[]{:S(2)}, u32[]{:S(2)}) %collective-permute-start.6) | collective-permute-done | bytes 1048608 | tf_op jit(solution)/shard_map/ppermute | solution.py:211
  77.5 1.2 copy-done.6
  78.7 1.2 copy-done.8
  79.9 23.1 %waves.3 = (f32[2,2,256,256]{3,2,1,0:T(8,128)}, f32[2,2,256,256]{3,2,1,0:T(8,128)}) custom-call(s32[2]{0:T(128)S(1)} %pad_add_fusion.3.info, f32[2,2,256,256]{3,2,1,0:T(8,128)S(1)} %copy-done.6, f32[2,2,256,256]{3,2,1,0:T(8,128)S(1)} %copy-done.8, f32[2,2,256,256]{3,2,1,0:T(8,128)S(1)} %collective-permute-done.4.refs_2_, ...), custom_call_target="tpu_custom_call" | custom-call | flops 8053063680 | bytes 8388608 | tf_op jit(solution)/shard_map/waves/pallas_call | solution.py:270
  103.1 2.3 %collective-permute-start.10 = (f32[2,2,256,256]{3,2,1,0:T(8,128)}, f32[2,2,256,256]{3,2,1,0:T(8,128)}, u32[]{:S(2)}, u32[]{:S(2)}) collective-permute-start(f32[2,2,256,256]{3,2,1,0:T(8,128)} %get-tuple-element.15), channel_id=1, source_target_pairs={{1,2},{3,4},{5,6},{7,8},{9,10},{11,12},{13,14},{15,0},{17,18},{19,... | collective-permute-start | bytes 3145736 | tf_op jit(solution)/shard_map/ppermute | solution.py:211
  105.3 2.3 %collective-permute-start.7 = (f32[2,2,256,256]{3,2,1,0:T(8,128)}, f32[2,2,256,256]{3,2,1,0:T(8,128)}, u32[]{:S(2)}, u32[]{:S(2)}) collective-permute-start(f32[2,2,256,256]{3,2,1,0:T(8,128)} %get-tuple-element.15), channel_id=1, source_target_pairs={{1,0},{3,2},{5,4},{7,6},{9,8},{11,10},{13,12},{15,14},{17,16},{19,... | collective-permute-start | bytes 3145736 | tf_op jit(solution)/shard_map/ppermute | solution.py:211
  107.6 2.5 %collective-permute-start.9 = (f32[2,2,256,256]{3,2,1,0:T(8,128)}, f32[2,2,256,256]{3,2,1,0:T(8,128)}, u32[]{:S(2)}, u32[]{:S(2)}) collective-permute-start(f32[2,2,256,256]{3,2,1,0:T(8,128)} %get-tuple-element.14.refs_1_), channel_id=1, source_target_pairs={{1,3},{3,5},{5,7},{7,9},{9,11},{11,13},{13,15},{15,1},{17,19},{19,... | collective-permute-start | bytes 3145736 | tf_op jit(solution)/shard_map/ppermute | solution.py:211
  111.0 5.4 %collective-permute-done.10.refs_6_ = f32[2,2,256,256]{3,2,1,0:T(8,128)} collective-permute-done((f32[2,2,256,256]{3,2,1,0:T(8,128)}, f32[2,2,256,256]{3,2,1,0:T(8,128)}, u32[]{:S(2)}, u32[]{:S(2)}) %collective-permute-start.10) | collective-permute-done | bytes 1048608 | tf_op jit(solution)/shard_map/ppermute | solution.py:211
  116.4 15.5 %collective-permute-done.9.refs_5_ = f32[2,2,256,256]{3,2,1,0:T(8,128)} collective-permute-done((f32[2,2,256,256]{3,2,1,0:T(8,128)}, f32[2,2,256,256]{3,2,1,0:T(8,128)}, u32[]{:S(2)}, u32[]{:S(2)}) %collective-permute-start.9) | collective-permute-done | bytes 1048608 | tf_op jit(solution)/shard_map/ppermute | solution.py:211
  131.9 5.6 %deposit.1 = (f32[2,256,1024]{2,1,0:T(8,128)}, f32[2,256,1024]{2,1,0:T(8,128)}) custom-call(s32[1]{0:T(128)} %bitcast.section, s32[4]{0:T(128)S(1)} %get-tuple-element.26.rows, s32[4]{0:T(128)S(1)} %get-tuple-element.27.cols, f32[2,2,256,256]{3,2,1,0:T(8,128)S(1)} %get-tuple-element.11.refs_0_, f32[2,2,256,256]{3,2,1,0:T(8,128)} %get-tuple-element.14.refs_1_, ...), custom_call_target="tpu_custom_call" | custom-call | tf_op jit(solution)/shard_map/deposit/pallas_call | solution.py:302
  (46 shorter events, 4.4 us)
Async XLA Ops:
  2.2 6.1 %collective-permute-start = (s32[2,2]{0,1:T(2,128)S(1)}, s32[2,2]{0,1:T(2,128)S(1)}, u32[]{:S(2)}, u32[]{:S(2)}) collective-permute-start(s32[2,2]{0,1:T(2,128)S(1)} %pad_add_fusion), channel_id=1, source_target_pairs={{0,2},{1,3},{2,4},{3,5},{4,6},{5,7},{6,8},{7,9},{8,10},{9,11},{10,... | collective-permute-start | bytes 56 | tf_op jit(solution)/shard_map/ppermute | solution.py:211
  9.6 1.6 %copy-start = (f32[2,256,1024]{2,1,0:T(8,128)S(1)}, f32[2,256,1024]{2,1,0:T(8,128)}, u32[]{:S(2)}) copy-start(f32[2,256,1024]{2,1,0:T(8,128)} %obj_r.3) | copy-start | bytes 6291460
  11.2 1.6 %copy-start.2 = (f32[2,256,1024]{2,1,0:T(8,128)S(1)}, f32[2,256,1024]{2,1,0:T(8,128)}, u32[]{:S(2)}) copy-start(f32[2,256,1024]{2,1,0:T(8,128)} %obj_i.3) | copy-start | bytes 6291460
  12.7 1.6 %copy-start.1 = (f32[2,256,1024]{2,1,0:T(8,128)S(1)}, f32[2,256,1024]{2,1,0:T(8,128)}, u32[]{:S(2)}) copy-start(f32[2,256,1024]{2,1,0:T(8,128)} %obj_r.3) | copy-start | bytes 6291460
  12.7 2.2 %copy-start.3 = (f32[2,256,1024]{2,1,0:T(8,128)S(1)}, f32[2,256,1024]{2,1,0:T(8,128)}, u32[]{:S(2)}) copy-start(f32[2,256,1024]{2,1,0:T(8,128)} %obj_i.3) | copy-start | bytes 6291460
  15.0 13.8 %copy-start.13 = (f32[2,63]{1,0:T(2,128)S(1)}, f32[2,63]{1,0:T(2,128)}, u32[]{:S(2)}) copy-start(f32[2,63]{1,0:T(2,128)} %param.11) | copy-start | bytes 1516
  17.9 1.0 copy-start.9
  18.9 32.1 %copy-start.5 = (f32[2,2,256,256]{3,2,1,0:T(8,128)}, f32[2,2,256,256]{3,2,1,0:T(8,128)S(1)}, u32[]{:S(2)}) copy-start(f32[2,2,256,256]{3,2,1,0:T(8,128)S(1)} %get-tuple-element.9.refs_0_) | copy-start | bytes 3145732
  18.9 15.3 %collective-permute-start.1 = (f32[2,2,256,256]{3,2,1,0:T(8,128)}, f32[2,2,256,256]{3,2,1,0:T(8,128)S(1)}, u32[]{:S(2)}, u32[]{:S(2)}) collective-permute-start(f32[2,2,256,256]{3,2,1,0:T(8,128)} %get-tuple-element.10), channel_id=1, source_target_pairs={{0,1},{1,0},{2,3},{3,2},{4,5},{5,4},{6,7},{7,6},{8,9},{9,8},{10,11... | collective-permute-start | bytes 3145736 | tf_op jit(solution)/shard_map/ppermute | solution.py:211
  20.4 13.8 %collective-permute-start.2 = (f32[2,2,256,256]{3,2,1,0:T(8,128)S(1)}, f32[2,2,256,256]{3,2,1,0:T(8,128)}, u32[]{:S(2)}, u32[]{:S(2)}) collective-permute-start(f32[2,2,256,256]{3,2,1,0:T(8,128)S(1)} %cut.2.rest_0_), channel_id=1, source_target_pairs={{0,14},{2,0},{4,2},{6,4},{8,6},{10,8},{12,10},{14,12},{16,30},{18,... | collective-permute-start | bytes 3145736 | tf_op jit(solution)/shard_map/ppermute | solution.py:211
  22.1 28.3 %collective-permute-start.3 = (f32[2,2,256,256]{3,2,1,0:T(8,128)S(1)}, f32[2,2,256,256]{3,2,1,0:T(8,128)}, u32[]{:S(2)}, u32[]{:S(2)}) collective-permute-start(f32[2,2,256,256]{3,2,1,0:T(8,128)S(1)} %cut.2.rest_0_), channel_id=1, source_target_pairs={{1,14},{3,0},{5,2},{7,4},{9,6},{11,8},{13,10},{15,12},{17,30},{19,... | collective-permute-start | bytes 3145736 | tf_op jit(solution)/shard_map/ppermute | solution.py:211
  29.1 1.7 %copy-start.10 = (f32[2,2,256,256]{3,2,1,0:T(8,128)S(1)}, f32[2,2,256,256]{3,2,1,0:T(8,128)}, u32[]{:S(2)}) copy-start(f32[2,2,256,256]{3,2,1,0:T(8,128)} %copy-done.9) | copy-start | bytes 3145732
  29.1 21.2 %copy-start.11 = (f32[2,256,256]{2,1,0:T(8,128)S(1)}, f32[2,256,256]{2,1,0:T(8,128)}, u32[]{:S(2)}) copy-start(f32[2,256,256]{2,1,0:T(8,128)} %refs_4_.3) | copy-start | bytes 1572868
  29.1 21.2 %copy-start.12 = (f32[2,256,256]{2,1,0:T(8,128)S(1)}, f32[2,256,256]{2,1,0:T(8,128)}, u32[]{:S(2)}) copy-start(f32[2,256,256]{2,1,0:T(8,128)} %refs_5_.3) | copy-start | bytes 1572868
  29.6 21.5 %copy-start.4 = (bf16[4,512,512]{2,1,0:T(8,128)(2,1)}, bf16[4,512,512]{2,1,0:T(8,128)(2,1)S(1)}, u32[]{:S(2)}) copy-start(bf16[4,512,512]{2,1,0:T(8,128)(2,1)S(1)} %band.1.refs_6_) | copy-start | bytes 6291460
  30.8 39.4 %collective-permute-start.4 = (f32[2,2,256,256]{3,2,1,0:T(8,128)S(1)}, f32[2,2,256,256]{3,2,1,0:T(8,128)S(1)}, u32[]{:S(2)}, u32[]{:S(2)}) collective-permute-start(f32[2,2,256,256]{3,2,1,0:T(8,128)S(1)} %copy-done.10), channel_id=1, source_target_pairs={{1,15},{3,1},{5,3},{7,5},{9,7},{11,9},{13,11},{15,13},{17,31},{19,... | collective-permute-start | bytes 3145736 | tf_op jit(solution)/shard_map/ppermute | solution.py:211
  32.9 37.2 %collective-permute-start.5 = (f32[2,2,256,256]{3,2,1,0:T(8,128)S(1)}, f32[2,2,256,256]{3,2,1,0:T(8,128)S(1)}, u32[]{:S(2)}, u32[]{:S(2)}) collective-permute-start(f32[2,2,256,256]{3,2,1,0:T(8,128)S(1)} %copy-done.10), channel_id=1, source_target_pairs={{0,15},{2,1},{4,3},{6,5},{8,7},{10,9},{12,11},{14,13},{16,31},{18,... | collective-permute-start | bytes 3145736 | tf_op jit(solution)/shard_map/ppermute | solution.py:211
  34.2 16.8 %copy-start.7 = (f32[2,2,256,256]{3,2,1,0:T(8,128)}, f32[2,2,256,256]{3,2,1,0:T(8,128)S(1)}, u32[]{:S(2)}) copy-start(f32[2,2,256,256]{3,2,1,0:T(8,128)S(1)} %collective-permute-done.1.refs_1_) | copy-start | bytes 3145732
  51.0 26.4 %collective-permute-start.6 = (f32[2,2,256,256]{3,2,1,0:T(8,128)}, f32[2,2,256,256]{3,2,1,0:T(8,128)S(1)}, u32[]{:S(2)}, u32[]{:S(2)}) collective-permute-start(f32[2,2,256,256]{3,2,1,0:T(8,128)} %get-tuple-element.13), channel_id=1, source_target_pairs={{0,1},{2,3},{4,5},{6,7},{8,9},{10,11},{12,13},{14,15},{16,17},{18,... | collective-permute-start | bytes 3145736 | tf_op jit(solution)/shard_map/ppermute | solution.py:211
  52.3 58.6 %collective-permute-start.11 = (f32[2,2,256,256]{3,2,1,0:T(8,128)}, f32[2,2,256,256]{3,2,1,0:T(8,128)S(1)}, u32[]{:S(2)}, u32[]{:S(2)}) collective-permute-start(f32[2,2,256,256]{3,2,1,0:T(8,128)} %get-tuple-element.13), channel_id=1, source_target_pairs={{0,3},{2,5},{4,7},{6,9},{8,11},{10,13},{12,15},{14,1},{16,19},{18,... | collective-permute-start | bytes 3145736 | tf_op jit(solution)/shard_map/ppermute | solution.py:211
  53.6 57.3 %collective-permute-start.8 = (f32[2,2,256,256]{3,2,1,0:T(8,128)S(1)}, f32[2,2,256,256]{3,2,1,0:T(8,128)}, u32[]{:S(2)}, u32[]{:S(2)}) collective-permute-start(f32[2,2,256,256]{3,2,1,0:T(8,128)S(1)} %get-tuple-element.11.refs_0_), channel_id=1, source_target_pairs={{0,2},{2,4},{4,6},{6,8},{8,10},{10,12},{12,14},{14,0},{16,18},{18,... | collective-permute-start | bytes 3145736 | tf_op jit(solution)/shard_map/ppermute | solution.py:211
  77.5 1.2 copy-start.6
  78.7 1.2 copy-start.8
  103.1 13.3 %collective-permute-start.10 = (f32[2,2,256,256]{3,2,1,0:T(8,128)}, f32[2,2,256,256]{3,2,1,0:T(8,128)}, u32[]{:S(2)}, u32[]{:S(2)}) collective-permute-start(f32[2,2,256,256]{3,2,1,0:T(8,128)} %get-tuple-element.15), channel_id=1, source_target_pairs={{1,2},{3,4},{5,6},{7,8},{9,10},{11,12},{13,14},{15,0},{17,18},{19,... | collective-permute-start | bytes 3145736 | tf_op jit(solution)/shard_map/ppermute | solution.py:211
  105.3 11.1 %collective-permute-start.7 = (f32[2,2,256,256]{3,2,1,0:T(8,128)}, f32[2,2,256,256]{3,2,1,0:T(8,128)}, u32[]{:S(2)}, u32[]{:S(2)}) collective-permute-start(f32[2,2,256,256]{3,2,1,0:T(8,128)} %get-tuple-element.15), channel_id=1, source_target_pairs={{1,0},{3,2},{5,4},{7,6},{9,8},{11,10},{13,12},{15,14},{17,16},{19,... | collective-permute-start | bytes 3145736 | tf_op jit(solution)/shard_map/ppermute | solution.py:211
  107.6 24.3 %collective-permute-start.9 = (f32[2,2,256,256]{3,2,1,0:T(8,128)}, f32[2,2,256,256]{3,2,1,0:T(8,128)}, u32[]{:S(2)}, u32[]{:S(2)}) collective-permute-start(f32[2,2,256,256]{3,2,1,0:T(8,128)} %get-tuple-element.14.refs_1_), channel_id=1, source_target_pairs={{1,3},{3,5},{5,7},{7,9},{9,11},{11,13},{13,15},{15,1},{17,19},{19,... | collective-permute-start | bytes 3145736 | tf_op jit(solution)/shard_map/ppermute | solution.py:211

commit v4 on v3

--- a/solution.py
+++ b/solution.py
@@ -281,7 +281,7 @@
                 pltpu.SemaphoreType.DMA((2 * depth,)),
                 pltpu.SemaphoreType.DMA((4,)),
             ],
-            compiler_params=pltpu.CompilerParams(vmem_limit_bytes=44 * 2**20),
+            compiler_params=pltpu.CompilerParams(vmem_limit_bytes=48 * 2**20),
             cost_estimate=pl.CostEstimate(
                 flops=(8 * depth + 4) * 24 * n**3, bytes_accessed=2**23, transcendentals=0
             ),
@@ -289,13 +289,13 @@
         )(info, own_s, own_o, *halos[phase], probe, intensity, bands, fourier, *after)
 
     terms = [waves(0)]
-    swapped = send(terms[0][1], 0, ((0, 1),))
-    terms.append(waves(1, swapped))
+    early = send(terms[0][0], 1, ((0, 0),))
+    terms.append(waves(1, early))
     pieces = [[], [], [], []]
     for k, (same, other) in enumerate(terms):
         pieces[0].append(same)
-        pieces[1].append(swapped if k == 0 else send(other, 0, ((k, 1 - k),)))
-        pieces[2].append(send(same, 1, ((k, k),)))
+        pieces[1].append(send(other, 0, ((k, 1 - k),)))
+        pieces[2].append(early if k == 0 else send(same, 1, ((k, k),)))
         pieces[3].append(send(other, 1, ((k, 1 - k),)))
     for k in (1, 3):
         pieces[k].reverse()

time: 138 us -> 135 us (0.978)
  waiting for transfers between devices: 62.4 us -> 57 us
  local copies, waits for them, and re-layouts: 11.7 us -> 16.7 us
  starting transfers between devices: 26.2 us -> 23.9 us
    ppermute x12, waiting for transfers between devices: 62.4 us -> 57 us  [send(): return lax.ppermute(x, ('pos', 'slab'), pairs)]
    unnamed x28 -> x36, local copies, waits for them, and re-layouts: 7.35 us -> 12.2 us
    ppermute x12, starting transfers between devices: 26.2 us -> 23.9 us  [send(): return lax.ppermute(x, ('pos', 'slab'), pairs)]
  transfers between devices with their start and end apart: 12 -> 12, of which waited for: 6 -> 5; matrix products, arithmetic and copies ran while one was open for 3% -> 2% of each run, Pallas kernels for 18% -> 18%
where the time goes in v4:
time: 135 us; the launch traced here: 134 us
  waiting for transfers between devices  57 us (42%)
  Pallas kernels  34.3 us (25%)
  starting transfers between devices  23.9 us (18%)
  local copies, waits for them, and re-layouts  16.7 us (12%)
  other arithmetic  1.74 us (1%)
    ppermute x12, waiting for transfers between devices, send(): return lax.ppermute(x, ('pos', 'slab'), pairs)  57 us
    pallas_call x2, Pallas kernels, waves(): pl.pallas_call(functools.partial(wave_kernel, phase), out_shape=[window]...  24.1 us
    ppermute x12, starting transfers between devices, send(): return lax.ppermute(x, ('pos', 'slab'), pairs)  23.9 us
    unnamed x36, local copies, waits for them, and re-layouts  12.2 us
    pallas_call x1, Pallas kernels, local(): pl.pallas_call(deposit_kernel, grid=(depth,), out_shape=[jax.ShapeDtypeSt...  5.43 us
    pallas_call x2, Pallas kernels, cut(): pl.pallas_call(cut_kernel, grid=(depth,), out_shape=[window] * count, in_...  4.44 us
  transfers between devices with their start and end apart: 12, of which 5 were waited for; matrix products, arithmetic and copies ran while one was open for 2% of the time, Pallas kernels for 18%

profile of v4, /device:TPU:1, one launch (start us, length us, event | category | flops | bytes accessed | tf_op | source)
XLA Modules:
  0.0 134.4 jit_solution(12364723363236415054)
XLA Ops:
  0.6 0.7 copy.12
  1.4 0.7 copy.13
  2.2 2.1 %collective-permute-start = (s32[2,2]{0,1:T(2,128)S(1)}, s32[2,2]{0,1:T(2,128)S(1)}, u32[]{:S(2)}, u32[]{:S(2)}) collective-permute-start(s32[2,2]{0,1:T(2,128)S(1)} %pad_add_fusion), channel_id=1, source_target_pairs={{0,2},{1,3},{2,4},{3,5},{4,6},{5,7},{6,8},{7,9},{8,10},{9,11},{10,... | collective-permute-start | bytes 56 | tf_op jit(solution)/shard_map/ppermute | solution.py:211
  5.1 3.2 %collective-permute-done = s32[2,2]{0,1:T(2,128)S(1)} collective-permute-done((s32[2,2]{0,1:T(2,128)S(1)}, s32[2,2]{0,1:T(2,128)S(1)}, u32[]{:S(2)}, u32[]{:S(2)}) %collective-permute-start) | collective-permute-done | bytes 48 | tf_op jit(solution)/shard_map/ppermute | solution.py:211
  9.6 1.6 %copy-done = f32[2,256,1024]{2,1,0:T(8,128)S(1)} copy-done((f32[2,256,1024]{2,1,0:T(8,128)S(1)}, f32[2,256,1024]{2,1,0:T(8,128)}, u32[]{:S(2)}) %copy-start) | copy-done | bytes 2097176
  11.2 1.6 %copy-done.2 = f32[2,256,1024]{2,1,0:T(8,128)S(1)} copy-done((f32[2,256,1024]{2,1,0:T(8,128)S(1)}, f32[2,256,1024]{2,1,0:T(8,128)}, u32[]{:S(2)}) %copy-start.2) | copy-done | bytes 2097176
  12.7 1.5 %cut.2.rest_0_ = f32[2,2,256,256]{3,2,1,0:T(8,128)S(1)} custom-call(s32[1]{0:T(128)} %bitcast.10.cols, f32[2,256,1024]{2,1,0:T(8,128)S(1)} %copy-done, f32[2,256,1024]{2,1,0:T(8,128)S(1)} %copy-done.2), custom_call_target="tpu_custom_call" | custom-call | bytes 8388608 | tf_op jit(solution)/shard_map/cut/pallas_call | solution.py:227
  15.0 2.9 %cut.3 = (f32[2,2,256,256]{3,2,1,0:T(8,128)S(1)}, f32[2,2,256,256]{3,2,1,0:T(8,128)S(1)}, f32[2,2,256,256]{3,2,1,0:T(8,128)}) custom-call(s32[3]{0:T(128)S(1)} %pad_add_fusion.4.cols, f32[2,256,1024]{2,1,0:T(8,128)S(1)} %copy-done.1, f32[2,256,1024]{2,1,0:T(8,128)S(1)} %copy-done.3, f32[2,2,256,256]{3,2,1,0:T(8,128)S(1)} %cut.2.rest_0_), custom_call_target="tpu_custom_call" | custom-call | bytes 8388608 | tf_op jit(solution)/shard_map/cut/pallas_call | solution.py:227
  17.9 1.0 copy-done.11
  18.9 1.5 %collective-permute-start.1 = (f32[2,2,256,256]{3,2,1,0:T(8,128)}, f32[2,2,256,256]{3,2,1,0:T(8,128)S(1)}, u32[]{:S(2)}, u32[]{:S(2)}) collective-permute-start(f32[2,2,256,256]{3,2,1,0:T(8,128)} %get-tuple-element.10), channel_id=1, source_target_pairs={{0,1},{1,0},{2,3},{3,2},{4,5},{5,4},{6,7},{7,6},{8,9},{9,8},{10,11... | collective-permute-start | bytes 3145736 | tf_op jit(solution)/shard_map/ppermute | solution.py:211
  20.4 1.7 %collective-permute-start.2 = (f32[2,2,256,256]{3,2,1,0:T(8,128)S(1)}, f32[2,2,256,256]{3,2,1,0:T(8,128)}, u32[]{:S(2)}, u32[]{:S(2)}) collective-permute-start(f32[2,2,256,256]{3,2,1,0:T(8,128)S(1)} %cut.2.rest_0_), channel_id=1, source_target_pairs={{0,14},{2,0},{4,2},{6,4},{8,6},{10,8},{12,10},{14,12},{16,30},{18,... | collective-permute-start | bytes 3145736 | tf_op jit(solution)/shard_map/ppermute | solution.py:211
  22.1 6.2 %collective-permute-start.3 = (f32[2,2,256,256]{3,2,1,0:T(8,128)S(1)}, f32[2,2,256,256]{3,2,1,0:T(8,128)}, u32[]{:S(2)}, u32[]{:S(2)}) collective-permute-start(f32[2,2,256,256]{3,2,1,0:T(8,128)S(1)} %cut.2.rest_0_), channel_id=1, source_target_pairs={{1,14},{3,0},{5,2},{7,4},{9,6},{11,8},{13,10},{15,12},{17,30},{19,... | collective-permute-start | bytes 3145736 | tf_op jit(solution)/shard_map/ppermute | solution.py:211
  29.7 1.3 copy-done.4
  31.7 2.1 %collective-permute-start.4 = (f32[2,2,256,256]{3,2,1,0:T(8,128)S(1)}, f32[2,2,256,256]{3,2,1,0:T(8,128)S(1)}, u32[]{:S(2)}, u32[]{:S(2)}) collective-permute-start(f32[2,2,256,256]{3,2,1,0:T(8,128)S(1)} %copy-done.12), channel_id=1, source_target_pairs={{1,15},{3,1},{5,3},{7,5},{9,7},{11,9},{13,11},{15,13},{17,31},{19,... | collective-permute-start | bytes 3145736 | tf_op jit(solution)/shard_map/ppermute | solution.py:211
  33.8 1.3 collective-permute-start.5
  35.1 15.2 %collective-permute-done.3.refs_3_ = f32[2,2,256,256]{3,2,1,0:T(8,128)} collective-permute-done((f32[2,2,256,256]{3,2,1,0:T(8,128)S(1)}, f32[2,2,256,256]{3,2,1,0:T(8,128)}, u32[]{:S(2)}, u32[]{:S(2)}) %collective-permute-start.3) | collective-permute-done | bytes 1048608 | tf_op jit(solution)/shard_map/ppermute | solution.py:211
  51.0 0.7 collective-permute-start.6
  51.8 1.3 collective-permute-start.11
  53.1 1.3 collective-permute-start.8
  54.4 15.8 %collective-permute-done.4.refs_2_ = f32[2,2,256,256]{3,2,1,0:T(8,128)S(1)} collective-permute-done((f32[2,2,256,256]{3,2,1,0:T(8,128)S(1)}, f32[2,2,256,256]{3,2,1,0:T(8,128)S(1)}, u32[]{:S(2)}, u32[]{:S(2)}) %collective-permute-start.4) | collective-permute-done | bytes 1048608 | tf_op jit(solution)/shard_map/ppermute | solution.py:211
  70.1 1.0 copy-done.16
  71.5 1.0 copy-done.5
  72.5 1.2 copy-done.8
  73.7 1.2 copy-done.10
  74.9 23.4 %waves.3 = (f32[2,2,256,256]{3,2,1,0:T(8,128)}, f32[2,2,256,256]{3,2,1,0:T(8,128)}) custom-call(s32[2]{0:T(128)S(1)} %pad_add_fusion.3.info, f32[2,2,256,256]{3,2,1,0:T(8,128)S(1)} %copy-done.8, f32[2,2,256,256]{3,2,1,0:T(8,128)S(1)} %copy-done.10, f32[2,2,256,256]{3,2,1,0:T(8,128)} %copy-done.16, f32[2,2,256,256]{3,2,1,0:T(8,128)} %copy-done.17, ...), custom_call_target="tpu_custom_call" | custom-call | flops 8053063680 | bytes 8388608 | tf_op jit(solution)/shard_map/waves/pallas_call | solution.py:270
  98.3 1.4 %collective-permute-start.10 = (f32[2,2,256,256]{3,2,1,0:T(8,128)}, f32[2,2,256,256]{3,2,1,0:T(8,128)S(1)}, u32[]{:S(2)}, u32[]{:S(2)}) collective-permute-start(f32[2,2,256,256]{3,2,1,0:T(8,128)} %get-tuple-element.14), channel_id=1, source_target_pairs={{1,2},{3,4},{5,6},{7,8},{9,10},{11,12},{13,14},{15,0},{17,18},{19,... | collective-permute-start | bytes 3145736 | tf_op jit(solution)/shard_map/ppermute | solution.py:211
  99.7 2.5 %collective-permute-start.7 = (f32[2,2,256,256]{3,2,1,0:T(8,128)}, f32[2,2,256,256]{3,2,1,0:T(8,128)}, u32[]{:S(2)}, u32[]{:S(2)}) collective-permute-start(f32[2,2,256,256]{3,2,1,0:T(8,128)} %get-tuple-element.14), channel_id=1, source_target_pairs={{1,0},{3,2},{5,4},{7,6},{9,8},{11,10},{13,12},{15,14},{17,16},{19,... | collective-permute-start | bytes 3145736 | tf_op jit(solution)/shard_map/ppermute | solution.py:211
  102.1 1.9 %collective-permute-start.9 = (f32[2,2,256,256]{3,2,1,0:T(8,128)}, f32[2,2,256,256]{3,2,1,0:T(8,128)}, u32[]{:S(2)}, u32[]{:S(2)}) collective-permute-start(f32[2,2,256,256]{3,2,1,0:T(8,128)} %get-tuple-element.13.refs_1_), channel_id=1, source_target_pairs={{1,3},{3,5},{5,7},{7,9},{9,11},{11,13},{13,15},{15,1},{17,19},{19,... | collective-permute-start | bytes 3145736 | tf_op jit(solution)/shard_map/ppermute | solution.py:211
  104.9 6.8 %collective-permute-done.10.refs_6_ = f32[2,2,256,256]{3,2,1,0:T(8,128)S(1)} collective-permute-done((f32[2,2,256,256]{3,2,1,0:T(8,128)}, f32[2,2,256,256]{3,2,1,0:T(8,128)S(1)}, u32[]{:S(2)}, u32[]{:S(2)}) %collective-permute-start.10) | collective-permute-done | bytes 1048608 | tf_op jit(solution)/shard_map/ppermute | solution.py:211
  111.7 16.1 %collective-permute-done.9.refs_5_ = f32[2,2,256,256]{3,2,1,0:T(8,128)} collective-permute-done((f32[2,2,256,256]{3,2,1,0:T(8,128)}, f32[2,2,256,256]{3,2,1,0:T(8,128)}, u32[]{:S(2)}, u32[]{:S(2)}) %collective-permute-start.9) | collective-permute-done | bytes 1048608 | tf_op jit(solution)/shard_map/ppermute | solution.py:211
  127.8 1.2 copy-done.6
  129.0 5.4 %deposit.1 = (f32[2,256,1024]{2,1,0:T(8,128)}, f32[2,256,1024]{2,1,0:T(8,128)}) custom-call(s32[1]{0:T(128)} %bitcast.section, s32[4]{0:T(128)S(1)} %get-tuple-element.26.rows, s32[4]{0:T(128)S(1)} %get-tuple-element.27.cols, f32[2,2,256,256]{3,2,1,0:T(8,128)S(1)} %get-tuple-element.11.refs_0_, f32[2,2,256,256]{3,2,1,0:T(8,128)} %get-tuple-element.13.refs_1_, ...), custom_call_target="tpu_custom_call" | custom-call | tf_op jit(solution)/shard_map/deposit/pallas_call | solution.py:302
  (54 shorter events, 6.9 us)
Async XLA Ops:
  2.2 6.1 %collective-permute-start = (s32[2,2]{0,1:T(2,128)S(1)}, s32[2,2]{0,1:T(2,128)S(1)}, u32[]{:S(2)}, u32[]{:S(2)}) collective-permute-start(s32[2,2]{0,1:T(2,128)S(1)} %pad_add_fusion), channel_id=1, source_target_pairs={{0,2},{1,3},{2,4},{3,5},{4,6},{5,7},{6,8},{7,9},{8,10},{9,11},{10,... | collective-permute-start | bytes 56 | tf_op jit(solution)/shard_map/ppermute | solution.py:211
  9.6 1.6 %copy-start = (f32[2,256,1024]{2,1,0:T(8,128)S(1)}, f32[2,256,1024]{2,1,0:T(8,128)}, u32[]{:S(2)}) copy-start(f32[2,256,1024]{2,1,0:T(8,128)} %obj_r.3) | copy-start | bytes 6291460
  11.2 1.6 %copy-start.2 = (f32[2,256,1024]{2,1,0:T(8,128)S(1)}, f32[2,256,1024]{2,1,0:T(8,128)}, u32[]{:S(2)}) copy-start(f32[2,256,1024]{2,1,0:T(8,128)} %obj_i.3) | copy-start | bytes 6291460
  12.7 1.6 %copy-start.1 = (f32[2,256,1024]{2,1,0:T(8,128)S(1)}, f32[2,256,1024]{2,1,0:T(8,128)}, u32[]{:S(2)}) copy-start(f32[2,256,1024]{2,1,0:T(8,128)} %obj_r.3) | copy-start | bytes 6291460
  12.7 2.2 %copy-start.3 = (f32[2,256,1024]{2,1,0:T(8,128)S(1)}, f32[2,256,1024]{2,1,0:T(8,128)}, u32[]{:S(2)}) copy-start(f32[2,256,1024]{2,1,0:T(8,128)} %obj_i.3) | copy-start | bytes 6291460
  15.0 13.9 %copy-start.15 = (f32[2,63]{1,0:T(2,128)S(1)}, f32[2,63]{1,0:T(2,128)}, u32[]{:S(2)}) copy-start(f32[2,63]{1,0:T(2,128)} %param.11) | copy-start | bytes 1516
  17.9 1.0 copy-start.11
  18.9 32.1 %copy-start.7 = (f32[2,2,256,256]{3,2,1,0:T(8,128)}, f32[2,2,256,256]{3,2,1,0:T(8,128)S(1)}, u32[]{:S(2)}) copy-start(f32[2,2,256,256]{3,2,1,0:T(8,128)S(1)} %get-tuple-element.9.refs_0_) | copy-start | bytes 3145732
  18.9 16.2 %collective-permute-start.1 = (f32[2,2,256,256]{3,2,1,0:T(8,128)}, f32[2,2,256,256]{3,2,1,0:T(8,128)S(1)}, u32[]{:S(2)}, u32[]{:S(2)}) collective-permute-start(f32[2,2,256,256]{3,2,1,0:T(8,128)} %get-tuple-element.10), channel_id=1, source_target_pairs={{0,1},{1,0},{2,3},{3,2},{4,5},{5,4},{6,7},{7,6},{8,9},{9,8},{10,11... | collective-permute-start | bytes 3145736 | tf_op jit(solution)/shard_map/ppermute | solution.py:211
  20.4 14.7 %collective-permute-start.2 = (f32[2,2,256,256]{3,2,1,0:T(8,128)S(1)}, f32[2,2,256,256]{3,2,1,0:T(8,128)}, u32[]{:S(2)}, u32[]{:S(2)}) collective-permute-start(f32[2,2,256,256]{3,2,1,0:T(8,128)S(1)} %cut.2.rest_0_), channel_id=1, source_target_pairs={{0,14},{2,0},{4,2},{6,4},{8,6},{10,8},{12,10},{14,12},{16,30},{18,... | collective-permute-start | bytes 3145736 | tf_op jit(solution)/shard_map/ppermute | solution.py:211
  22.1 28.2 %collective-permute-start.3 = (f32[2,2,256,256]{3,2,1,0:T(8,128)S(1)}, f32[2,2,256,256]{3,2,1,0:T(8,128)}, u32[]{:S(2)}, u32[]{:S(2)}) collective-permute-start(f32[2,2,256,256]{3,2,1,0:T(8,128)S(1)} %cut.2.rest_0_), channel_id=1, source_target_pairs={{1,14},{3,0},{5,2},{7,4},{9,6},{11,8},{13,10},{15,12},{17,30},{19,... | collective-permute-start | bytes 3145736 | tf_op jit(solution)/shard_map/ppermute | solution.py:211
  29.2 2.5 %copy-start.12 = (f32[2,2,256,256]{3,2,1,0:T(8,128)S(1)}, f32[2,2,256,256]{3,2,1,0:T(8,128)}, u32[]{:S(2)}) copy-start(f32[2,2,256,256]{3,2,1,0:T(8,128)} %copy-done.11) | copy-start | bytes 3145732
  29.2 21.1 %copy-start.13 = (f32[2,256,256]{2,1,0:T(8,128)S(1)}, f32[2,256,256]{2,1,0:T(8,128)}, u32[]{:S(2)}) copy-start(f32[2,256,256]{2,1,0:T(8,128)} %refs_4_.3) | copy-start | bytes 1572868
  29.2 21.1 %copy-start.14 = (f32[2,256,256]{2,1,0:T(8,128)S(1)}, f32[2,256,256]{2,1,0:T(8,128)}, u32[]{:S(2)}) copy-start(f32[2,256,256]{2,1,0:T(8,128)} %refs_5_.3) | copy-start | bytes 1572868
  29.6 1.3 copy-start.4
  31.7 38.4 %collective-permute-start.4 = (f32[2,2,256,256]{3,2,1,0:T(8,128)S(1)}, f32[2,2,256,256]{3,2,1,0:T(8,128)S(1)}, u32[]{:S(2)}, u32[]{:S(2)}) collective-permute-start(f32[2,2,256,256]{3,2,1,0:T(8,128)S(1)} %copy-done.12), channel_id=1, source_target_pairs={{1,15},{3,1},{5,3},{7,5},{9,7},{11,9},{13,11},{15,13},{17,31},{19,... | collective-permute-start | bytes 3145736 | tf_op jit(solution)/shard_map/ppermute | solution.py:211
  33.8 36.3 %collective-permute-start.5 = (f32[2,2,256,256]{3,2,1,0:T(8,128)S(1)}, f32[2,2,256,256]{3,2,1,0:T(8,128)S(1)}, u32[]{:S(2)}, u32[]{:S(2)}) collective-permute-start(f32[2,2,256,256]{3,2,1,0:T(8,128)S(1)} %copy-done.12), channel_id=1, source_target_pairs={{0,15},{2,1},{4,3},{6,5},{8,7},{10,9},{12,11},{14,13},{16,31},{18,... | collective-permute-start | bytes 3145736 | tf_op jit(solution)/shard_map/ppermute | solution.py:211
  35.1 15.9 %copy-start.9 = (f32[2,2,256,256]{3,2,1,0:T(8,128)}, f32[2,2,256,256]{3,2,1,0:T(8,128)S(1)}, u32[]{:S(2)}) copy-start(f32[2,2,256,256]{3,2,1,0:T(8,128)S(1)} %collective-permute-done.1.refs_1_) | copy-start | bytes 3145732
  51.0 19.1 %collective-permute-start.6 = (f32[2,2,256,256]{3,2,1,0:T(8,128)S(1)}, f32[2,2,256,256]{3,2,1,0:T(8,128)S(1)}, u32[]{:S(2)}, u32[]{:S(2)}) collective-permute-start(f32[2,2,256,256]{3,2,1,0:T(8,128)S(1)} %get-tuple-element.11.refs_0_), channel_id=1, source_target_pairs={{0,2},{2,4},{4,6},{6,8},{8,10},{10,12},{12,14},{14,0},{16,18},{18,... | collective-permute-start | bytes 3145736 | tf_op jit(solution)/shard_map/ppermute | solution.py:211
  51.8 53.1 %collective-permute-start.11 = (f32[2,2,256,256]{3,2,1,0:T(8,128)}, f32[2,2,256,256]{3,2,1,0:T(8,128)S(1)}, u32[]{:S(2)}, u32[]{:S(2)}) collective-permute-start(f32[2,2,256,256]{3,2,1,0:T(8,128)} %get-tuple-element.15), channel_id=1, source_target_pairs={{0,3},{2,5},{4,7},{6,9},{8,11},{10,13},{12,15},{14,1},{16,19},{18,... | collective-permute-start | bytes 3145736 | tf_op jit(solution)/shard_map/ppermute | solution.py:211
  53.1 51.8 %collective-permute-start.8 = (f32[2,2,256,256]{3,2,1,0:T(8,128)}, f32[2,2,256,256]{3,2,1,0:T(8,128)}, u32[]{:S(2)}, u32[]{:S(2)}) collective-permute-start(f32[2,2,256,256]{3,2,1,0:T(8,128)} %get-tuple-element.15), channel_id=1, source_target_pairs={{0,1},{2,3},{4,5},{6,7},{8,9},{10,11},{12,13},{14,15},{16,17},{18,... | collective-permute-start | bytes 3145736 | tf_op jit(solution)/shard_map/ppermute | solution.py:211
  70.1 1.0 copy-start.16
  70.1 1.4 %copy-start.17 = (f32[2,2,256,256]{3,2,1,0:T(8,128)}, f32[2,2,256,256]{3,2,1,0:T(8,128)S(1)}, u32[]{:S(2)}) copy-start(f32[2,2,256,256]{3,2,1,0:T(8,128)S(1)} %collective-permute-done.5.refs_3_) | copy-start | bytes 3145732
  71.5 1.0 copy-start.5
  72.5 1.2 copy-start.8
  73.7 1.2 copy-start.10
  98.3 13.3 %collective-permute-start.10 = (f32[2,2,256,256]{3,2,1,0:T(8,128)}, f32[2,2,256,256]{3,2,1,0:T(8,128)S(1)}, u32[]{:S(2)}, u32[]{:S(2)}) collective-permute-start(f32[2,2,256,256]{3,2,1,0:T(8,128)} %get-tuple-element.14), channel_id=1, source_target_pairs={{1,2},{3,4},{5,6},{7,8},{9,10},{11,12},{13,14},{15,0},{17,18},{19,... | collective-permute-start | bytes 3145736 | tf_op jit(solution)/shard_map/ppermute | solution.py:211
  99.7 12.0 %collective-permute-start.7 = (f32[2,2,256,256]{3,2,1,0:T(8,128)}, f32[2,2,256,256]{3,2,1,0:T(8,128)}, u32[]{:S(2)}, u32[]{:S(2)}) collective-permute-start(f32[2,2,256,256]{3,2,1,0:T(8,128)} %get-tuple-element.14), channel_id=1, source_target_pairs={{1,0},{3,2},{5,4},{7,6},{9,8},{11,10},{13,12},{15,14},{17,16},{19,... | collective-permute-start | bytes 3145736 | tf_op jit(solution)/shard_map/ppermute | solution.py:211
  102.1 25.6 %collective-permute-start.9 = (f32[2,2,256,256]{3,2,1,0:T(8,128)}, f32[2,2,256,256]{3,2,1,0:T(8,128)}, u32[]{:S(2)}, u32[]{:S(2)}) collective-permute-start(f32[2,2,256,256]{3,2,1,0:T(8,128)} %get-tuple-element.13.refs_1_), channel_id=1, source_target_pairs={{1,3},{3,5},{5,7},{7,9},{9,11},{11,13},{13,15},{15,1},{17,19},{19,... | collective-permute-start | bytes 3145736 | tf_op jit(solution)/shard_map/ppermute | solution.py:211
  127.8 1.2 copy-start.6

commit v5 on v2

--- a/solution.py
+++ b/solution.py
@@ -71,6 +71,20 @@
             out[ri, 0] = pltpu.roll(wide, lax.rem(span - shift, span), 1)[:, :n]
 
 
+def band_kernel(ring, out):
+    n = out.shape[-1] // 2
+
+    def toeplitz(k):
+        rows = jnp.broadcast_to(ring[k : k + 1, :], (n, 2 * n))
+        return pltpu.roll(rows, 0, 1, stride=1, stride_axis=0)[:, :n]
+
+    for k, kr, ki in ((0, toeplitz(0), -toeplitz(1)), (2, toeplitz(2), toeplitz(3))):
+        for r0, c0, block in ((0, 0, kr), (0, n, ki), (n, 0, -ki), (n, n, kr)):
+            hi, lo = halves(block)
+            out[k, r0 : r0 + n, c0 : c0 + n] = hi
+            out[k + 1, r0 : r0 + n, c0 : c0 + n] = lo
+
+
 def wave_kernel(phase, info, *refs):
     if phase > 0:
         refs = refs[:11] + refs[12:]
@@ -81,8 +95,8 @@
 
 
 def wave_body(
-    info, own_s, own_o, halo_s, halo_o, probe, ring, intensity, ch, cl, dh, dl,
-    term_s, term_o, patch, waves, ah, al, bh, bl,
+    info, own_s, own_o, halo_s, halo_o, probe, bands, intensity, ch, cl, dh, dl,
+    term_s, term_o, patch, waves,
 ):
     n = probe.shape[-1]
     depth = own_s.shape[1]
@@ -95,16 +109,7 @@
                 merged = jnp.where(from_next, halo[ri, d], own[ri, d])
                 patch[where * depth + d, ri] = pltpu.roll(merged, unroll_by, 0)
 
-    def toeplitz(k):
-        rows = jnp.broadcast_to(ring[k : k + 1, :], (n, 2 * n))
-        return pltpu.roll(rows, 0, 1, stride=1, stride_axis=0)[:, :n]
-
-    for high, low, kr, ki in ((ah, al, toeplitz(0), -toeplitz(1)), (bh, bl, toeplitz(2), toeplitz(3))):
-        for r0, c0, block in ((0, 0, kr), (0, n, ki), (n, 0, -ki), (n, n, kr)):
-            hi, lo = halves(block)
-            high[r0 : r0 + n, c0 : c0 + n] = hi
-            low[r0 : r0 + n, c0 : c0 + n] = lo
-
+    ah, al, bh, bl = (bands.at[k] for k in range(4))
     waves[0] = probe[...]
     slices = 2 * depth
 
@@ -203,14 +208,6 @@
             name="cut",
         )(places, obj_real, obj_imag, *after)
 
-    (first_halo,) = cut(tile_before[1, :1])
-    halos = [[send(first_halo, -1, ((0, 0),)), send(first_halo, -1, ((1, 0),))]]
-    second_halo, own_s, own_o = cut(
-        jnp.concatenate([tile_before[1, 1:], mine[1]]), first_halo
-    )
-    halos.append([send(second_halo, -1, ((1, 1),)), send(second_halo, -1, ((0, 1),))])
-    own_o = send(own_o, 0, ((0, 1), (1, 0)))
-
     half = (taps.shape[1] - 1) // 2
     gap = jnp.zeros((2, 2 * n - taps.shape[1]), F32)
     back = taps[:, ::-1]
@@ -221,8 +218,23 @@
         ],
         0,
     )
+    bands = pl.pallas_call(
+        band_kernel,
+        out_shape=jax.ShapeDtypeStruct((4, 2 * n, 2 * n), BF16),
+        in_specs=[VMEM],
+        out_specs=VMEM,
+        compiler_params=pltpu.CompilerParams(vmem_limit_bytes=40 * 2**20),
+        name="band",
+    )(ring)
+    (first_halo,) = cut(tile_before[1, :1], bands)
+    halos = [[send(first_halo, -1, ((0, 0),)), send(first_halo, -1, ((1, 0),))]]
+    second_halo, own_s, own_o = cut(
+        jnp.concatenate([tile_before[1, 1:], mine[1]]), first_halo
+    )
+    halos.append([send(second_halo, -1, ((1, 1),)), send(second_halo, -1, ((0, 1),))])
+    own_o = send(own_o, 0, ((0, 1), (1, 0)))
+
     info = jnp.stack([section, rows[0]]).astype(jnp.int32)
-    square = pltpu.VMEM((2 * n, 2 * n), BF16)
     constants = fourier_blocks(n)
 
     def waves(phase, *after):
@@ -234,22 +246,22 @@
             scratch_shapes=[
                 pltpu.VMEM((2 * depth, 2, n, n), F32),
                 pltpu.VMEM((2 * depth + 1, 2, n, n), F32),
-                square, square, square, square,
             ],
             compiler_params=pltpu.CompilerParams(vmem_limit_bytes=48 * 2**20),
             cost_estimate=pl.CostEstimate(
                 flops=(8 * depth + 4) * 24 * n**3, bytes_accessed=2**23, transcendentals=0
             ),
             name="waves",
-        )(info, own_s, own_o, *halos[phase], probe, ring, intensity, *constants, *after)
+        )(info, own_s, own_o, *halos[phase], probe, bands, intensity, *constants, *after)
 
     terms = [waves(0)]
-    terms.append(waves(1, terms[0][0]))
+    early = send(terms[0][0], 1, ((0, 0),))
+    terms.append(waves(1, early))
     pieces = [[], [], [], []]
     for k, (same, other) in enumerate(terms):
         pieces[0].append(same)
         pieces[1].append(send(other, 0, ((k, 1 - k),)))
-        pieces[2].append(send(same, 1, ((k, k),)))
+        pieces[2].append(early if k == 0 else send(same, 1, ((k, k),)))
         pieces[3].append(send(other, 1, ((k, 1 - k),)))
     for k in (1, 3):
         pieces[k].reverse()

time: 132 us -> 136 us (1.030)
  the two profiles are of different devices: /device:TPU:0 before, /device:TPU:1 now
where the time goes in v5:
time: 136 us
  waiting for transfers between devices  52.2 us (38%)
  Pallas kernels  38 us (28%)
  starting transfers between devices  29.2 us (21%)
  local copies, waits for them, and re-layouts  13.4 us (10%)
  other arithmetic  1.81 us (1%)
    ppermute x12, waiting for transfers between devices, send(): return lax.ppermute(x, ('pos', 'slab'), pairs)  52.2 us
    ppermute x12, starting transfers between devices, send(): return lax.ppermute(x, ('pos', 'slab'), pairs)  29.2 us
    pallas_call x2, Pallas kernels, waves(): pl.pallas_call(functools.partial(wave_kernel, phase), out_shape=[window]...  28.4 us
    unnamed x36, local copies, waits for them, and re-layouts  7.25 us
    pallas_call x1, Pallas kernels, local(): pl.pallas_call(deposit_kernel, grid=(depth,), out_shape=[jax.ShapeDtypeSt...  5.49 us
    pallas_call x2, Pallas kernels, cut(): pl.pallas_call(cut_kernel, grid=(depth,), out_shape=[window] * count, in_...  3.73 us
  transfers between devices with their start and end apart: 12, of which 5 were waited for; matrix products, arithmetic and copies ran while one was open for 4% of the time, Pallas kernels for 21%

profile of v5, /device:TPU:1, one launch (start us, length us, event | category | flops | bytes accessed | tf_op | source)
XLA Modules:
  0.0 135.5 jit_solution(11876404217456589356)
XLA Ops:
  0.6 0.9 copy.15
  1.5 0.7 copy.16
  2.3 2.1 %collective-permute-start = (s32[2,2]{0,1:T(2,128)S(1)}, s32[2,2]{0,1:T(2,128)S(1)}, u32[]{:S(2)}, u32[]{:S(2)}) collective-permute-start(s32[2,2]{0,1:T(2,128)S(1)} %pad_add_fusion), channel_id=1, source_target_pairs={{0,2},{1,3},{2,4},{3,5},{4,6},{5,7},{6,8},{7,9},{8,10},{9,11},{10,... | collective-permute-start | bytes 56 | tf_op jit(solution)/shard_map/ppermute | solution.py:184
  4.4 0.8 fusion.1
  5.2 0.8 fusion.2
  7.5 0.9 collective-permute-done
  9.1 0.7 pad_add_fusion.4.cols
  9.8 1.6 %copy-done.1 = f32[2,256,1024]{2,1,0:T(8,128)S(1)} copy-done((f32[2,256,1024]{2,1,0:T(8,128)S(1)}, f32[2,256,1024]{2,1,0:T(8,128)}, u32[]{:S(2)}) %copy-start.1) | copy-done | bytes 2097176
  11.4 1.5 %cut.2.rest_0_ = f32[2,2,256,256]{3,2,1,0:T(8,128)S(1)} custom-call(s32[1]{0:T(128)} %bitcast.10.cols, f32[2,256,1024]{2,1,0:T(8,128)S(1)} %copy-done, f32[2,256,1024]{2,1,0:T(8,128)S(1)} %copy-done.1, bf16[4,512,512]{2,1,0:T(8,128)(2,1)S(1)} %band.1.rest_0_.refs_5_), custom_call_target="tpu_custom_call" | custom-call | bytes 8388608 | tf_op jit(solution)/shard_map/cut/pallas_call | solution.py:200
  13.0 2.2 %cut.3 = (f32[2,2,256,256]{3,2,1,0:T(8,128)S(1)}, f32[2,2,256,256]{3,2,1,0:T(8,128)S(1)}, f32[2,2,256,256]{3,2,1,0:T(8,128)S(1)}) custom-call(s32[3]{0:T(128)S(1)} %pad_add_fusion.4.cols, f32[2,256,1024]{2,1,0:T(8,128)S(1)} %copy-done, f32[2,256,1024]{2,1,0:T(8,128)S(1)} %copy-done.2, f32[2,2,256,256]{3,2,1,0:T(8,128)S(1)} %cut.2.rest_0_), custom_call_target="tpu_custom_call" | custom-call | bytes 8388608 | tf_op jit(solution)/shard_map/cut/pallas_call | solution.py:200
  15.3 1.0 copy-done.6
  16.3 1.5 %collective-permute-start.1 = (f32[2,2,256,256]{3,2,1,0:T(8,128)S(1)}, f32[2,2,256,256]{3,2,1,0:T(8,128)S(1)}, u32[]{:S(2)}, u32[]{:S(2)}) collective-permute-start(f32[2,2,256,256]{3,2,1,0:T(8,128)S(1)} %get-tuple-element.10), channel_id=1, source_target_pairs={{0,1},{1,0},{2,3},{3,2},{4,5},{5,4},{6,7},{7,6},{8,9},{9,8},{10,11... | collective-permute-start | bytes 3145736 | tf_op jit(solution)/shard_map/ppermute | solution.py:184
  18.5 6.5 %collective-permute-start.3 = (f32[2,2,256,256]{3,2,1,0:T(8,128)S(1)}, f32[2,2,256,256]{3,2,1,0:T(8,128)S(1)}, u32[]{:S(2)}, u32[]{:S(2)}) collective-permute-start(f32[2,2,256,256]{3,2,1,0:T(8,128)S(1)} %cut.2.rest_0_), channel_id=1, source_target_pairs={{1,14},{3,0},{5,2},{7,4},{9,6},{11,8},{13,10},{15,12},{17,30},{19,... | collective-permute-start | bytes 3145736 | tf_op jit(solution)/shard_map/ppermute | solution.py:184
  25.6 0.7 pad_add_fusion.3.info
  26.3 3.0 %collective-permute-start.4 = (f32[2,2,256,256]{3,2,1,0:T(8,128)S(1)}, f32[2,2,256,256]{3,2,1,0:T(8,128)S(1)}, u32[]{:S(2)}, u32[]{:S(2)}) collective-permute-start(f32[2,2,256,256]{3,2,1,0:T(8,128)S(1)} %get-tuple-element.12), channel_id=1, source_target_pairs={{1,15},{3,1},{5,3},{7,5},{9,7},{11,9},{13,11},{15,13},{17,31},{19,... | collective-permute-start | bytes 3145736 | tf_op jit(solution)/shard_map/ppermute | solution.py:184
  29.4 1.3 collective-permute-start.5
  30.7 17.3 %collective-permute-done.3.refs_3_ = f32[2,2,256,256]{3,2,1,0:T(8,128)S(1)} collective-permute-done((f32[2,2,256,256]{3,2,1,0:T(8,128)S(1)}, f32[2,2,256,256]{3,2,1,0:T(8,128)S(1)}, u32[]{:S(2)}, u32[]{:S(2)}) %collective-permute-start.3) | collective-permute-done | bytes 1048608 | tf_op jit(solution)/shard_map/ppermute | solution.py:184
  48.0 0.9 copy-done.17
  49.0 3.8 %waves.2 = (f32[2,2,256,256]{3,2,1,0:T(8,128)S(1)}, f32[2,2,256,256]{3,2,1,0:T(8,128)}) custom-call(s32[2]{0:T(128)S(1)} %pad_add_fusion.3.info, f32[2,2,256,256]{3,2,1,0:T(8,128)} %copy-done.6, f32[2,2,256,256]{3,2,1,0:T(8,128)} %copy-done.13, f32[2,2,256,256]{3,2,1,0:T(8,128)} %copy-done.16, f32[2,2,256,256]{3,2,1,0:T(8,128)} %copy-done.17, ...), custom_call_target="tpu_custom_call" | custom-call | flops 8053063680 | bytes 8388608 | tf_op jit(solution)/shard_map/waves/pallas_call | solution.py:241
  53.5 1.3 collective-permute-start.11
  54.8 1.3 collective-permute-start.8
  56.1 11.4 %collective-permute-done.4.refs_2_ = f32[2,2,256,256]{3,2,1,0:T(8,128)S(1)} collective-permute-done((f32[2,2,256,256]{3,2,1,0:T(8,128)S(1)}, f32[2,2,256,256]{3,2,1,0:T(8,128)S(1)}, u32[]{:S(2)}, u32[]{:S(2)}) %collective-permute-start.4) | collective-permute-done | bytes 1048608 | tf_op jit(solution)/shard_map/ppermute | solution.py:184
  67.5 1.0 copy-done.14
  68.9 1.0 copy-done.4
  69.9 24.6 %waves.3 = (f32[2,2,256,256]{3,2,1,0:T(8,128)}, f32[2,2,256,256]{3,2,1,0:T(8,128)}) custom-call(s32[2]{0:T(128)S(1)} %pad_add_fusion.3.info, f32[2,2,256,256]{3,2,1,0:T(8,128)} %copy-done.6, f32[2,2,256,256]{3,2,1,0:T(8,128)} %copy-done.13, f32[2,2,256,256]{3,2,1,0:T(8,128)} %copy-done.14, f32[2,2,256,256]{3,2,1,0:T(8,128)} %copy-done.15, ...), custom_call_target="tpu_custom_call" | custom-call | flops 8053063680 | bytes 8388608 | tf_op jit(solution)/shard_map/waves/pallas_call | solution.py:241
  94.5 4.2 %collective-permute-start.10 = (f32[2,2,256,256]{3,2,1,0:T(8,128)}, f32[2,2,256,256]{3,2,1,0:T(8,128)S(1)}, u32[]{:S(2)}, u32[]{:S(2)}) collective-permute-start(f32[2,2,256,256]{3,2,1,0:T(8,128)} %get-tuple-element.14), channel_id=1, source_target_pairs={{1,2},{3,4},{5,6},{7,8},{9,10},{11,12},{13,14},{15,0},{17,18},{19,... | collective-permute-start | bytes 3145736 | tf_op jit(solution)/shard_map/ppermute | solution.py:184
  98.8 4.6 %collective-permute-start.7 = (f32[2,2,256,256]{3,2,1,0:T(8,128)}, f32[2,2,256,256]{3,2,1,0:T(8,128)}, u32[]{:S(2)}, u32[]{:S(2)}) collective-permute-start(f32[2,2,256,256]{3,2,1,0:T(8,128)} %get-tuple-element.14), channel_id=1, source_target_pairs={{1,0},{3,2},{5,4},{7,6},{9,8},{11,10},{13,12},{15,14},{17,16},{19,... | collective-permute-start | bytes 3145736 | tf_op jit(solution)/shard_map/ppermute | solution.py:184
  103.3 1.9 %collective-permute-start.9 = (f32[2,2,256,256]{3,2,1,0:T(8,128)}, f32[2,2,256,256]{3,2,1,0:T(8,128)}, u32[]{:S(2)}, u32[]{:S(2)}) collective-permute-start(f32[2,2,256,256]{3,2,1,0:T(8,128)} %get-tuple-element.13.refs_1_), channel_id=1, source_target_pairs={{1,3},{3,5},{5,7},{7,9},{9,11},{11,13},{13,15},{15,1},{17,19},{19,... | collective-permute-start | bytes 3145736 | tf_op jit(solution)/shard_map/ppermute | solution.py:184
  106.1 5.4 %collective-permute-done.10.refs_6_ = f32[2,2,256,256]{3,2,1,0:T(8,128)S(1)} collective-permute-done((f32[2,2,256,256]{3,2,1,0:T(8,128)}, f32[2,2,256,256]{3,2,1,0:T(8,128)S(1)}, u32[]{:S(2)}, u32[]{:S(2)}) %collective-permute-start.10) | collective-permute-done | bytes 1048608 | tf_op jit(solution)/shard_map/ppermute | solution.py:184
  111.5 17.3 %collective-permute-done.9.refs_5_ = f32[2,2,256,256]{3,2,1,0:T(8,128)} collective-permute-done((f32[2,2,256,256]{3,2,1,0:T(8,128)}, f32[2,2,256,256]{3,2,1,0:T(8,128)}, u32[]{:S(2)}, u32[]{:S(2)}) %collective-permute-start.9) | collective-permute-done | bytes 1048608 | tf_op jit(solution)/shard_map/ppermute | solution.py:184
  128.8 1.2 copy-done.5
  130.0 5.5 %deposit.1 = (f32[2,256,1024]{2,1,0:T(8,128)}, f32[2,256,1024]{2,1,0:T(8,128)}) custom-call(s32[1]{0:T(128)} %bitcast.section, s32[4]{0:T(128)S(1)} %get-tuple-element.26.rows, s32[4]{0:T(128)S(1)} %get-tuple-element.27.cols, f32[2,2,256,256]{3,2,1,0:T(8,128)S(1)} %get-tuple-element.11.refs_0_, f32[2,2,256,256]{3,2,1,0:T(8,128)} %get-tuple-element.13.refs_1_, ...), custom_call_target="tpu_custom_call" | custom-call | tf_op jit(solution)/shard_map/deposit/pallas_call | solution.py:268
  (54 shorter events, 5.6 us)
Async XLA Ops:
  0.6 9.2 %copy-start = (f32[2,256,1024]{2,1,0:T(8,128)S(1)}, f32[2,256,1024]{2,1,0:T(8,128)}, u32[]{:S(2)}) copy-start(f32[2,256,1024]{2,1,0:T(8,128)} %obj_r.3) | copy-start | bytes 6291460
  2.3 6.1 %collective-permute-start = (s32[2,2]{0,1:T(2,128)S(1)}, s32[2,2]{0,1:T(2,128)S(1)}, u32[]{:S(2)}, u32[]{:S(2)}) collective-permute-start(s32[2,2]{0,1:T(2,128)S(1)} %pad_add_fusion), channel_id=1, source_target_pairs={{0,2},{1,3},{2,4},{3,5},{4,6},{5,7},{6,8},{7,9},{8,10},{9,11},{10,... | collective-permute-start | bytes 56 | tf_op jit(solution)/shard_map/ppermute | solution.py:184
  7.5 5.4 %copy-start.3 = (bf16[4,512,512]{2,1,0:T(8,128)(2,1)}, bf16[4,512,512]{2,1,0:T(8,128)(2,1)S(1)}, u32[]{:S(2)}) copy-start(bf16[4,512,512]{2,1,0:T(8,128)(2,1)S(1)} %band.1.rest_0_.refs_5_) | copy-start | bytes 6291460
  9.8 1.6 %copy-start.1 = (f32[2,256,1024]{2,1,0:T(8,128)S(1)}, f32[2,256,1024]{2,1,0:T(8,128)}, u32[]{:S(2)}) copy-start(f32[2,256,1024]{2,1,0:T(8,128)} %obj_i.3) | copy-start | bytes 6291460
  11.4 1.6 %copy-start.2 = (f32[2,256,1024]{2,1,0:T(8,128)S(1)}, f32[2,256,1024]{2,1,0:T(8,128)}, u32[]{:S(2)}) copy-start(f32[2,256,1024]{2,1,0:T(8,128)} %obj_i.3) | copy-start | bytes 6291460
  13.0 35.9 %copy-start.7 = (f32[2,256,256]{2,1,0:T(8,128)S(1)}, f32[2,256,256]{2,1,0:T(8,128)}, u32[]{:S(2)}) copy-start(f32[2,256,256]{2,1,0:T(8,128)} %refs_4_.3) | copy-start | bytes 1572868
  13.0 35.9 %copy-start.8 = (f32[2,256,256]{2,1,0:T(8,128)S(1)}, f32[2,256,256]{2,1,0:T(8,128)}, u32[]{:S(2)}) copy-start(f32[2,256,256]{2,1,0:T(8,128)} %refs_6_.3) | copy-start | bytes 1572868
  13.0 35.9 %copy-start.9 = (bf16[512,512]{1,0:T(8,128)(2,1)S(1)}, bf16[512,512]{1,0:T(8,128)(2,1)}, u32[]{:S(2)}) copy-start(bf16[512,512]{1,0:T(8,128)(2,1)} %constant.20.clone.refs_7_) | copy-start | bytes 1572868
  13.0 35.9 %copy-start.10 = (bf16[512,512]{1,0:T(8,128)(2,1)S(1)}, bf16[512,512]{1,0:T(8,128)(2,1)}, u32[]{:S(2)}) copy-start(bf16[512,512]{1,0:T(8,128)(2,1)} %constant.21.clone.refs_8_) | copy-start | bytes 1572868
  13.0 35.9 %copy-start.11 = (bf16[512,512]{1,0:T(8,128)(2,1)S(1)}, bf16[512,512]{1,0:T(8,128)(2,1)}, u32[]{:S(2)}) copy-start(bf16[512,512]{1,0:T(8,128)(2,1)} %constant.22.clone.refs_9_) | copy-start | bytes 1572868
  13.0 35.9 %copy-start.12 = (bf16[512,512]{1,0:T(8,128)(2,1)S(1)}, bf16[512,512]{1,0:T(8,128)(2,1)}, u32[]{:S(2)}) copy-start(bf16[512,512]{1,0:T(8,128)(2,1)} %constant.23.clone.refs_10_) | copy-start | bytes 1572868
  15.3 1.0 copy-start.6
  16.3 14.4 %collective-permute-start.1 = (f32[2,2,256,256]{3,2,1,0:T(8,128)S(1)}, f32[2,2,256,256]{3,2,1,0:T(8,128)S(1)}, u32[]{:S(2)}, u32[]{:S(2)}) collective-permute-start(f32[2,2,256,256]{3,2,1,0:T(8,128)S(1)} %get-tuple-element.10), channel_id=1, source_target_pairs={{0,1},{1,0},{2,3},{3,2},{4,5},{5,4},{6,7},{7,6},{8,9},{9,8},{10,11... | collective-permute-start | bytes 3145736 | tf_op jit(solution)/shard_map/ppermute | solution.py:184
  17.8 12.9 %collective-permute-start.2 = (f32[2,2,256,256]{3,2,1,0:T(8,128)S(1)}, f32[2,2,256,256]{3,2,1,0:T(8,128)S(1)}, u32[]{:S(2)}, u32[]{:S(2)}) collective-permute-start(f32[2,2,256,256]{3,2,1,0:T(8,128)S(1)} %cut.2.rest_0_), channel_id=1, source_target_pairs={{0,14},{2,0},{4,2},{6,4},{8,6},{10,8},{12,10},{14,12},{16,30},{18,... | collective-permute-start | bytes 3145736 | tf_op jit(solution)/shard_map/ppermute | solution.py:184
  18.5 29.5 %collective-permute-start.3 = (f32[2,2,256,256]{3,2,1,0:T(8,128)S(1)}, f32[2,2,256,256]{3,2,1,0:T(8,128)S(1)}, u32[]{:S(2)}, u32[]{:S(2)}) collective-permute-start(f32[2,2,256,256]{3,2,1,0:T(8,128)S(1)} %cut.2.rest_0_), channel_id=1, source_target_pairs={{1,14},{3,0},{5,2},{7,4},{9,6},{11,8},{13,10},{15,12},{17,30},{19,... | collective-permute-start | bytes 3145736 | tf_op jit(solution)/shard_map/ppermute | solution.py:184
  26.3 41.2 %collective-permute-start.4 = (f32[2,2,256,256]{3,2,1,0:T(8,128)S(1)}, f32[2,2,256,256]{3,2,1,0:T(8,128)S(1)}, u32[]{:S(2)}, u32[]{:S(2)}) collective-permute-start(f32[2,2,256,256]{3,2,1,0:T(8,128)S(1)} %get-tuple-element.12), channel_id=1, source_target_pairs={{1,15},{3,1},{5,3},{7,5},{9,7},{11,9},{13,11},{15,13},{17,31},{19,... | collective-permute-start | bytes 3145736 | tf_op jit(solution)/shard_map/ppermute | solution.py:184
  29.4 38.1 %collective-permute-start.5 = (f32[2,2,256,256]{3,2,1,0:T(8,128)S(1)}, f32[2,2,256,256]{3,2,1,0:T(8,128)S(1)}, u32[]{:S(2)}, u32[]{:S(2)}) collective-permute-start(f32[2,2,256,256]{3,2,1,0:T(8,128)S(1)} %get-tuple-element.12), channel_id=1, source_target_pairs={{0,15},{2,1},{4,3},{6,5},{8,7},{10,9},{12,11},{14,13},{16,31},{18,... | collective-permute-start | bytes 3145736 | tf_op jit(solution)/shard_map/ppermute | solution.py:184
  30.7 17.3 %copy-start.13 = (f32[2,2,256,256]{3,2,1,0:T(8,128)}, f32[2,2,256,256]{3,2,1,0:T(8,128)S(1)}, u32[]{:S(2)}) copy-start(f32[2,2,256,256]{3,2,1,0:T(8,128)S(1)} %collective-permute-done.1.refs_1_) | copy-start | bytes 3145732
  30.7 17.3 %copy-start.16 = (f32[2,2,256,256]{3,2,1,0:T(8,128)}, f32[2,2,256,256]{3,2,1,0:T(8,128)S(1)}, u32[]{:S(2)}) copy-start(f32[2,2,256,256]{3,2,1,0:T(8,128)S(1)} %collective-permute-done.2.refs_2_) | copy-start | bytes 3145732
  48.0 1.0 copy-start.17
  52.8 14.7 %collective-permute-start.6 = (f32[2,2,256,256]{3,2,1,0:T(8,128)S(1)}, f32[2,2,256,256]{3,2,1,0:T(8,128)S(1)}, u32[]{:S(2)}, u32[]{:S(2)}) collective-permute-start(f32[2,2,256,256]{3,2,1,0:T(8,128)S(1)} %get-tuple-element.11.refs_0_), channel_id=1, source_target_pairs={{0,2},{2,4},{4,6},{6,8},{8,10},{10,12},{12,14},{14,0},{16,18},{18,... | collective-permute-start | bytes 3145736 | tf_op jit(solution)/shard_map/ppermute | solution.py:184
  53.5 52.6 %collective-permute-start.11 = (f32[2,2,256,256]{3,2,1,0:T(8,128)}, f32[2,2,256,256]{3,2,1,0:T(8,128)S(1)}, u32[]{:S(2)}, u32[]{:S(2)}) collective-permute-start(f32[2,2,256,256]{3,2,1,0:T(8,128)} %get-tuple-element.15), channel_id=1, source_target_pairs={{0,3},{2,5},{4,7},{6,9},{8,11},{10,13},{12,15},{14,1},{16,19},{18,... | collective-permute-start | bytes 3145736 | tf_op jit(solution)/shard_map/ppermute | solution.py:184
  54.8 51.3 %collective-permute-start.8 = (f32[2,2,256,256]{3,2,1,0:T(8,128)}, f32[2,2,256,256]{3,2,1,0:T(8,128)}, u32[]{:S(2)}, u32[]{:S(2)}) collective-permute-start(f32[2,2,256,256]{3,2,1,0:T(8,128)} %get-tuple-element.15), channel_id=1, source_target_pairs={{0,1},{2,3},{4,5},{6,7},{8,9},{10,11},{12,13},{14,15},{16,17},{18,... | collective-permute-start | bytes 3145736 | tf_op jit(solution)/shard_map/ppermute | solution.py:184
  67.5 1.0 copy-start.14
  67.5 1.4 %copy-start.15 = (f32[2,2,256,256]{3,2,1,0:T(8,128)}, f32[2,2,256,256]{3,2,1,0:T(8,128)S(1)}, u32[]{:S(2)}) copy-start(f32[2,2,256,256]{3,2,1,0:T(8,128)S(1)} %collective-permute-done.5.refs_3_) | copy-start | bytes 3145732
  68.9 1.0 copy-start.4
  94.5 17.0 %collective-permute-start.10 = (f32[2,2,256,256]{3,2,1,0:T(8,128)}, f32[2,2,256,256]{3,2,1,0:T(8,128)S(1)}, u32[]{:S(2)}, u32[]{:S(2)}) collective-permute-start(f32[2,2,256,256]{3,2,1,0:T(8,128)} %get-tuple-element.14), channel_id=1, source_target_pairs={{1,2},{3,4},{5,6},{7,8},{9,10},{11,12},{13,14},{15,0},{17,18},{19,... | collective-permute-start | bytes 3145736 | tf_op jit(solution)/shard_map/ppermute | solution.py:184
  98.8 12.7 %collective-permute-start.7 = (f32[2,2,256,256]{3,2,1,0:T(8,128)}, f32[2,2,256,256]{3,2,1,0:T(8,128)}, u32[]{:S(2)}, u32[]{:S(2)}) collective-permute-start(f32[2,2,256,256]{3,2,1,0:T(8,128)} %get-tuple-element.14), channel_id=1, source_target_pairs={{1,0},{3,2},{5,4},{7,6},{9,8},{11,10},{13,12},{15,14},{17,16},{19,... | collective-permute-start | bytes 3145736 | tf_op jit(solution)/shard_map/ppermute | solution.py:184
  103.3 25.5 %collective-permute-start.9 = (f32[2,2,256,256]{3,2,1,0:T(8,128)}, f32[2,2,256,256]{3,2,1,0:T(8,128)}, u32[]{:S(2)}, u32[]{:S(2)}) collective-permute-start(f32[2,2,256,256]{3,2,1,0:T(8,128)} %get-tuple-element.13.refs_1_), channel_id=1, source_target_pairs={{1,3},{3,5},{5,7},{7,9},{9,11},{11,13},{13,15},{15,1},{17,19},{19,... | collective-permute-start | bytes 3145736 | tf_op jit(solution)/shard_map/ppermute | solution.py:184
  128.8 1.2 copy-start.5
